TPU v7x, 256 devices: a whole 4x4x8 slice. The times are simulated.
256 devices in a mesh: ctx: 32 (over z_hi, x, y), tensor: 8 (over z_lo, core).
Axes of the slice: x: 4, y: 4, z: 8 (z_hi: 2, z_lo: 4; z = z_hi * 4 + z_lo), core: 2. Of those that a mesh axis runs over, the one named last changes fastest.
Arguments:
- query_rows: bfloat16 [4096, 8192], P('ctx', 'tensor'), may hold values from -6 to 6
- key_rows: bfloat16 [4096, 8192], P('ctx', 'tensor'), may hold values from -6 to 6
- value_rows: bfloat16 [4096, 8192], P('ctx', 'tensor'), may hold values from -6 to 6
- grad_rows: bfloat16 [4096, 8192], P('ctx', 'tensor'), may hold values from -6 to 6
- residues: float32 [512, 16], replicated, may hold values from -0.25 to 0.25
- decay_rates: float32 [512, 16], replicated, may hold values from 0.00012207031 to 0.05
Outputs:
- operator_out: bfloat16 [4096, 8192], P('ctx', 'tensor')
- grad_query: bfloat16 [4096, 8192], P('ctx', 'tensor')
- grad_key: bfloat16 [4096, 8192], P('ctx', 'tensor')
- grad_value: bfloat16 [4096, 8192], P('ctx', 'tensor')
- grad_residues: float32 [512, 16], replicated
- grad_rates: float32 [512, 16], replicated
All inputs are finite; a program needn't handle non-finite values.
Results may differ from a plain program's by a relative error of at most 0.013.
Values may be sent and summed in bfloat16 or wider, within the bound.
A program may use at most 192 MiB of HBM per device.

v0:
```python
import jax
import jax.numpy as jnp
import numpy as np
from jax import lax
from jax.sharding import PartitionSpec as P

W = 8192
FILTERS = 512
ORDER = 16
BLOCK = 64


exact_mode = lax.Precision.HIGHEST


def lag_table(block_len):
    index_grid = np.arange(block_len)
    lag_grid = (
        index_grid[:, None, None] - index_grid[None, :, None] == index_grid[None, None, :]
    ).astype(np.float32)
    return jnp.asarray(lag_grid)


def forward_join(rate_c):

    def forward_joined(former, latter):
        span_a, first_a, second_a = former
        span_b, first_b, second_b = latter
        factor = jnp.exp(-rate_c * span_b)
        return (
            span_a + span_b,
            factor * first_a + first_b,
            factor * (second_a + span_b * first_a) + second_b,
        )

    return forward_joined


def backward_join(rate_c):

    def backward_joined(former, latter):
        span_a, state_a = former
        span_b, state_b = latter
        factor = jnp.exp(-rate_c * span_b)
        return (span_a + span_b, factor * state_a + state_b)

    return backward_joined


def local_terms(u_blocks, dz_blocks, res_c, rate_c):
    block_len = u_blocks.shape[1]
    steps_f = jnp.arange(block_len, dtype=jnp.float32)
    powers = jnp.exp(-rate_c[:, :, None] * steps_f)
    reverse_pow = powers[:, :, ::-1]
    lag_grid = lag_table(block_len)
    kernel = jnp.einsum("cr,crj->cj", res_c, powers, precision=exact_mode)
    toeplitz = jnp.einsum("cj,tsj->cts", kernel, lag_grid, precision=exact_mode)
    conv_out = jnp.einsum("cts,bsc->btc", toeplitz, u_blocks, precision=exact_mode)
    back_out = jnp.einsum("cts,btc->bsc", toeplitz, dz_blocks, precision=exact_mode)
    pair_sums = jnp.einsum("btc,bsc->cts", dz_blocks, u_blocks, precision=exact_mode)
    lagged = jnp.einsum("cts,tsj->cj", pair_sums, lag_grid, precision=exact_mode)
    grad_res = jnp.einsum("cj,crj->cr", lagged, powers, precision=exact_mode)
    grad_sum = jnp.einsum("cj,crj->cr", lagged * steps_f, powers, precision=exact_mode)
    ends_one = jnp.einsum("bsc,crs->bcr", u_blocks, reverse_pow, precision=exact_mode)
    ends_two = jnp.einsum(
        "bsc,crs->bcr", u_blocks, reverse_pow * steps_f[::-1], precision=exact_mode
    )
    starts_one = jnp.einsum("btc,crt->bcr", dz_blocks, powers, precision=exact_mode)
    starts_two = jnp.einsum("btc,crt->bcr", dz_blocks, powers * steps_f, precision=exact_mode)
    return (
        conv_out,
        back_out,
        grad_res,
        grad_sum,
        ends_one,
        ends_two,
        starts_one,
        starts_two,
        powers,
    )


def block_states(local_out, rate_c):
    block_count = local_out[0].shape[0]
    block_len = local_out[0].shape[1]
    span_list = jnp.full((block_count, 1, 1), float(block_len), jnp.float32)
    span_out, incl_one, incl_two = lax.associative_scan(
        forward_join(rate_c), (span_list, local_out[4], local_out[5])
    )
    span_back, incl_back = lax.associative_scan(
        backward_join(rate_c), (span_list, local_out[6]), reverse=True
    )
    return (incl_one, incl_two, incl_back)


def apply_states(local_out, block_scan, res_c, rate_c, dev_one, dev_back):
    conv_out, back_out, grad_res, grad_sum, ends_one, ends_two, starts_one, starts_two, powers = (
        local_out
    )
    incl_one, incl_two, incl_back = block_scan
    block_count = conv_out.shape[0]
    block_len = conv_out.shape[1]
    zero_row = jnp.zeros_like(incl_one[:1])
    prior_one = jnp.concatenate([zero_row, incl_one[:-1]], axis=0)
    prior_two = jnp.concatenate([zero_row, incl_two[:-1]], axis=0)
    after_back = jnp.concatenate([incl_back[1:], zero_row], axis=0)
    offsets = (jnp.arange(block_count, dtype=jnp.float32) * block_len)[:, None, None]
    total_len = float(block_count * block_len)
    decay_in = jnp.exp(-rate_c * offsets)
    state_one = prior_one + decay_in * dev_one
    state_two = prior_two + decay_in * (offsets * dev_one)
    state_back = after_back + jnp.exp(-rate_c * (total_len - offsets - block_len)) * dev_back
    single = jnp.exp(-rate_c)
    ahead_pow = powers * single[:, :, None]
    behind_pow = powers[:, :, ::-1] * single[:, :, None]
    conv_out = conv_out + jnp.einsum(
        "bcr,crt->btc", res_c * state_one, ahead_pow, precision=exact_mode
    )
    back_out = back_out + jnp.einsum(
        "bcr,crs->bsc", res_c * state_back, behind_pow, precision=exact_mode
    )
    grad_res = grad_res + single * jnp.sum(state_one * starts_one, axis=0)
    grad_sum = grad_sum + single * jnp.sum(
        state_two * starts_one + state_one * (starts_two + starts_one), axis=0
    )
    return (conv_out, back_out, grad_res, -res_c * grad_sum)


def per_device(query_rows, key_rows, value_rows, grad_rows, residues, decay_rates):
    row_count, chan_count = query_rows.shape
    group_size = W // FILTERS
    product_rows = (query_rows.astype(jnp.float32) * key_rows.astype(jnp.float32)).astype(
        jnp.bfloat16
    )
    dz_rows = (grad_rows.astype(jnp.float32) * value_rows.astype(jnp.float32)).astype(jnp.bfloat16)
    res_all = jnp.repeat(residues, group_size, axis=0)
    rate_all = jnp.repeat(decay_rates, group_size, axis=0)
    tensor_pos = lax.axis_index("tensor")
    moved_u, moved_dz = (
        lax.all_to_all(product_rows, "ctx", split_axis=1, concat_axis=0, tiled=True),
        lax.all_to_all(dz_rows, "ctx", split_axis=1, concat_axis=0, tiled=True),
    )
    length, narrow = moved_u.shape
    first_chan = tensor_pos * chan_count + lax.axis_index("ctx") * narrow
    res_c = lax.dynamic_slice_in_dim(res_all, first_chan, narrow, 0)
    rate_c = lax.dynamic_slice_in_dim(rate_all, first_chan, narrow, 0)
    block_count = length // BLOCK
    u_blocks = moved_u.astype(jnp.float32).reshape(block_count, BLOCK, narrow)
    dz_blocks = moved_dz.astype(jnp.float32).reshape(block_count, BLOCK, narrow)
    local_out = local_terms(u_blocks, dz_blocks, res_c, rate_c)
    block_scan = block_states(local_out, rate_c)
    zero_state = jnp.zeros((narrow, ORDER), jnp.float32)
    conv_out, back_out, grad_res, grad_rate = apply_states(
        local_out, block_scan, res_c, rate_c, zero_state, zero_state
    )
    conv_send = conv_out.reshape(length, narrow).astype(jnp.bfloat16)
    back_send = back_out.reshape(length, narrow).astype(jnp.bfloat16)
    conv_rows, back_rows = (
        lax.all_to_all(conv_send, "ctx", split_axis=0, concat_axis=1, tiled=True),
        lax.all_to_all(back_send, "ctx", split_axis=0, concat_axis=1, tiled=True),
    )
    conv_f = conv_rows.astype(jnp.float32)
    back_f = back_rows.astype(jnp.float32)
    operator_out = (value_rows.astype(jnp.float32) * conv_f).astype(jnp.bfloat16)
    grad_value = (grad_rows.astype(jnp.float32) * conv_f).astype(jnp.bfloat16)
    grad_query = (back_f * key_rows.astype(jnp.float32)).astype(jnp.bfloat16)
    grad_key = (back_f * query_rows.astype(jnp.float32)).astype(jnp.bfloat16)
    filter_ids = (first_chan + jnp.arange(narrow, dtype=jnp.int32)) // group_size
    onehot = (filter_ids[:, None] == jnp.arange(FILTERS, dtype=jnp.int32)[None, :]).astype(
        jnp.float32
    )
    sum_res = jnp.einsum("cf,cr->fr", onehot, grad_res, precision=exact_mode)
    sum_rate = jnp.einsum("cf,cr->fr", onehot, grad_rate, precision=exact_mode)
    grad_residues, grad_rates = lax.psum((sum_res, sum_rate), ("ctx", "tensor"))
    return (operator_out, grad_query, grad_key, grad_value, grad_residues, grad_rates)


def solution(mesh):
    placed = (
        P("ctx", "tensor"),
        P("ctx", "tensor"),
        P("ctx", "tensor"),
        P("ctx", "tensor"),
        P(),
        P(),
    )
    return jax.shard_map(
        per_device,
        mesh=mesh,
        in_specs=placed,
        out_specs=(
            P("ctx", "tensor"),
            P("ctx", "tensor"),
            P("ctx", "tensor"),
            P("ctx", "tensor"),
            P(),
            P(),
        ),
        check_vma=False,
    )
```

profile of v0, /device:TPU:1, one launch (start us, length us, event | category | flops | bytes accessed | tf_op | source)
XLA Modules:
  0.0 524.7 jit_solution(4115261534123584326)
XLA Ops:
  7.2 1.1 copy.181
  8.3 1.2 copy.205
  10.3 14.5 %all-to-all-start.2 = ((bf16[128,32,32]{0,2,1:T(8,128)(2,1)}), bf16[128,32,32]{0,2,1:T(8,128)(2,1)S(1)}, u32[]{:S(2)}, u32[]{:S(2)}) async-start(bf16[128,32,32]{0,2,1:T(8,128)(2,1)} %bitcast.16), calls=%async_computation.2 | async-start | bytes 524288 | tf_op jit(solution)/shard_map/all_to_all | solution.py:141
  28.8 7.4 %fusion.75 = f32[32,64,64]{2,0,1:T(8,128)S(1)} fusion(f32[32,64,1]{1,0,2:T(8,128)S(1)} %bitcast.118, f32[64,64,64]{2,1,0:T(8,128)} %constant.62.clone), kind=kOutput, calls=%fused_computation.175 | convolution fusion | flops 100663296 | bytes 1581056 | tf_op jit(solution)/shard_map/cj,tsj->cts/dot_general | solution.py:57
  41.0 11.2 %pad.262 = f32[64,32,16]{1,2,0:T(8,128)S(1)} pad(f32[32,32,16]{1,2,0:T(8,128)} %add.356, f32[]{:T(128)} %constant.19.clone.1), padding=1_0_1x0_0_0x0_0_0 | pad | bytes 196612
  54.0 11.2 %pad.185 = f32[63,32,16]{1,2,0:T(8,128)S(1)} pad(f32[32,32,16]{1,2,0:T(8,128)} %pad_maximum_fusion.1, f32[]{:T(128)} %constant.19.clone.1), padding=0_0_1x0_0_0x0_0_0 | pad | bytes 194564 | tf_op jit(solution)/shard_map/slice | solution.py:106
  67.7 1.3 convolution_bitcast_fusion.2
  69.0 1.9 fusion.2
  72.0 11.2 %all-to-all-start.3 = ((bf16[32,128,32]{1,2,0:T(8,128)(2,1)}), bf16[32,128,32]{1,2,0:T(8,128)(2,1)S(1)}, u32[]{:S(2)}, u32[]{:S(2)}) async-start(bf16[32,128,32]{1,2,0:T(8,128)(2,1)} %copy.211), calls=%async_computation.3 | async-start | bytes 524288 | tf_op jit(solution)/shard_map/all_to_all | solution.py:160
  83.3 1.8 copy.183
  85.1 9.9 %all-to-all-done.3 = bf16[32,128,32]{1,2,0:T(8,128)(2,1)S(1)} async-done(((bf16[32,128,32]{1,2,0:T(8,128)(2,1)}), bf16[32,128,32]{1,2,0:T(8,128)(2,1)S(1)}, u32[]{:S(2)}, u32[]{:S(2)}) %all-to-all-start.3) | async-done | bytes 262176 | tf_op jit(solution)/shard_map/all_to_all | solution.py:160
  95.0 1.8 fusion.9
  96.8 3.9 all-to-all-start
  105.7 6.8 %all-to-all-done = bf16[128,32,32]{0,2,1:T(8,128)(2,1)S(1)} async-done(((bf16[128,32,32]{0,2,1:T(8,128)(2,1)}), bf16[128,32,32]{0,2,1:T(8,128)(2,1)S(1)}, u32[]{:S(2)}, u32[]{:S(2)}) %all-to-all-start) | async-done | bytes 262176 | tf_op jit(solution)/shard_map/all_to_all | solution.py:140
  114.9 1.6 fusion.20
  116.6 1.2 copy.215
  117.8 1.1 slice_add_fusion
  126.2 1.9 pad.116
  128.2 1.9 pad.117
  130.1 1.9 pad.141
  132.0 1.3 pad_maximum_fusion.14
  133.3 1.9 pad.140
  135.3 1.4 add.331
  136.7 1.5 fusion.51
  138.1 1.4 add.379
  139.5 1.3 slice.367
  140.8 1.3 pad_maximum_fusion.9
  142.1 3.2 pad.118
  145.3 3.2 pad.119
  148.5 1.4 pad_maximum_fusion.11
  149.9 3.2 pad.142
  153.1 3.2 pad.143
  156.3 1.5 add.333
  157.8 1.6 fusion.46
  159.4 1.5 add.382
  161.5 1.3 slice.366
  163.4 1.3 pad_maximum_fusion.6
  164.7 2.8 pad.120
  167.5 4.7 pad.121
  172.2 4.7 pad.145
  176.8 1.4 pad_maximum_fusion.8
  178.3 4.6 pad.144
  182.9 1.6 add.335
  184.5 1.8 fusion.41
  187.3 1.3 slice.365
  188.6 1.4 pad_maximum_fusion.3
  190.0 5.6 %pad.122 = f32[32,32,16]{1,2,0:T(8,128)S(1)} pad(f32[16,32,16]{1,2,0:T(8,128)} %pad_maximum_fusion.3, f32[]{:T(128)} %constant.19.clone.1), padding=0_1_1x0_0_0x0_0_0 | pad | bytes 98308 | tf_op jit(solution)/shard_map/pad | solution.py:87
  195.6 8.4 %pad.123 = f32[32,32,16]{1,2,0:T(8,128)} pad(f32[16,32,16]{1,2,0:T(8,128)} %add.335, f32[]{:T(128)} %constant.19.clone.1), padding=1_0_1x0_0_0x0_0_0 | pad | bytes 98308 | tf_op jit(solution)/shard_map/pad | solution.py:87
  204.0 1.6 pad_maximum_fusion.5
  205.6 8.4 %pad.146 = f32[32,32,16]{1,2,0:T(8,128)} pad(f32[16,32,16]{1,2,0:T(8,128)} %pad_maximum_fusion.5, f32[]{:T(128)} %constant.19.clone.1), padding=0_1_1x0_0_0x0_0_0 | pad | bytes 98308 | tf_op jit(solution)/shard_map/pad | solution.py:87
  214.0 5.5 %pad.147 = f32[32,32,16]{1,2,0:T(8,128)} pad(f32[16,32,16]{1,2,0:T(8,128)S(1)} %add.385, f32[]{:T(128)} %constant.19.clone.1), padding=1_0_1x0_0_0x0_0_0 | pad | bytes 98308 | tf_op jit(solution)/shard_map/pad | solution.py:87
  219.5 1.7 add.337
  221.2 2.3 fusion.29
  224.2 1.3 fusion.77
  225.6 2.6 convolution_bitcast_fusion.3
  229.4 10.3 %pad.183 = f32[63,32,16]{1,2,0:T(8,128)} pad(f32[32,32,16]{1,2,0:T(8,128)S(1)} %pad_maximum_fusion, f32[]{:T(128)} %constant.19.clone.1), padding=0_0_1x0_0_0x0_0_0 | pad | bytes 194564 | tf_op jit(solution)/shard_map/slice | solution.py:104
  240.1 10.4 %pad.187 = f32[63,32,16]{1,2,0:T(8,128)} pad(f32[32,32,16]{1,2,0:T(8,128)S(1)} %pad_maximum_fusion.2, f32[]{:T(128)} %constant.19.clone.1), padding=0_0_1x0_0_0x0_0_0 | pad | bytes 194564 | tf_op jit(solution)/shard_map/slice | solution.py:105
  250.4 3.5 bitcast_multiply_fusion
  256.1 2.0 fusion.3
  259.1 4.8 all-to-all-start.1
  266.5 9.4 %all-to-all-done.1 = bf16[32,128,32]{1,2,0:T(8,128)(2,1)S(1)} async-done(((bf16[32,128,32]{1,2,0:T(8,128)(2,1)}), bf16[32,128,32]{1,2,0:T(8,128)(2,1)S(1)}, u32[]{:S(2)}, u32[]{:S(2)}) %all-to-all-start.1) | async-done | bytes 262176 | tf_op jit(solution)/shard_map/all_to_all | solution.py:159
  277.7 237.4 %all-reduce.42.cloned.1.call-done = (f32[512,16]{0,1:T(8,128)}, f32[512,16]{0,1:T(8,128)}) async-done(((f32[512,16]{0,1:T(8,128)}, f32[512,16]{0,1:T(8,128)}), (f32[512,16]{0,1:T(8,128)}, f32[512,16]{0,1:T(8,128)})) %all-reduce.42.cloned.1.call-update) | async-done | bytes 65552 | tf_op jit(solution)/shard_map/psum | solution.py:174
  515.1 1.4 copy.247
  516.4 1.4 copy.248
  (200 shorter events, 41.0 us)
Async XLA Ops:
  7.2 17.7 %copy-start.36 = (f32[512,16]{0,1:T(8,128)S(1)}, f32[512,16]{0,1:T(8,128)}, u32[]{:S(2)}) copy-start(f32[512,16]{0,1:T(8,128)} %param.11) | copy-start | bytes 98308
  7.2 17.8 %copy-start.37 = (f32[512,16]{0,1:T(8,128)S(1)}, f32[512,16]{0,1:T(8,128)}, u32[]{:S(2)}) copy-start(f32[512,16]{0,1:T(8,128)} %param.12) | copy-start | bytes 98308
  8.3 17.1 %copy-start.2 = (bf16[128,1024]{0,1:T(8,128)(2,1)}, bf16[128,1024]{0,1:T(8,128)(2,1)S(1)}, u32[]{:S(2)}) copy-start(bf16[128,1024]{0,1:T(8,128)(2,1)S(1)} %copy.181) | copy-start | bytes 786436
  9.6 15.9 %copy-start.4 = (bf16[128,1024]{0,1:T(8,128)(2,1)}, bf16[128,1024]{0,1:T(8,128)(2,1)S(1)}, u32[]{:S(2)}) copy-start(bf16[128,1024]{0,1:T(8,128)(2,1)S(1)} %copy.205) | copy-start | bytes 786436
  10.3 26.5 %all-to-all-start.2 = ((bf16[128,32,32]{0,2,1:T(8,128)(2,1)}), bf16[128,32,32]{0,2,1:T(8,128)(2,1)S(1)}, u32[]{:S(2)}, u32[]{:S(2)}) async-start(bf16[128,32,32]{0,2,1:T(8,128)(2,1)} %bitcast.16), calls=%async_computation.2 | async-start | bytes 524288 | tf_op jit(solution)/shard_map/all_to_all | solution.py:141
  25.7 10.4 %copy-start.33 = (f32[32,16]{1,0:T(8,128)}, f32[32,16]{1,0:T(8,128)S(1)}, u32[]{:S(2)}) copy-start(f32[32,16]{1,0:T(8,128)S(1)} %get-tuple-element.88) | copy-start | bytes 6148
  25.8 43.2 %copy-start.25 = (f32[32,16]{1,0:T(8,128)}, f32[32,16]{1,0:T(8,128)S(1)}, u32[]{:S(2)}) copy-start(f32[32,16]{1,0:T(8,128)S(1)} %get-tuple-element.40) | copy-start | bytes 6148
  27.2 90.6 %copy-start.21 = (f32[32,16]{0,1:T(8,128)}, f32[32,16]{0,1:T(8,128)S(1)}, u32[]{:S(2)}) copy-start(f32[32,16]{0,1:T(8,128)S(1)} %copy.190) | copy-start | bytes 6148
  27.3 12.0 %copy-start.22 = (f32[32,16]{0,1:T(8,128)}, f32[32,16]{0,1:T(8,128)S(1)}, u32[]{:S(2)}) copy-start(f32[32,16]{0,1:T(8,128)S(1)} %copy.192) | copy-start | bytes 6148
  27.3 11.7 %copy-start.23 = (f32[32,16]{0,1:T(8,128)}, f32[32,16]{0,1:T(8,128)S(1)}, u32[]{:S(2)}) copy-start(f32[32,16]{0,1:T(8,128)S(1)} %copy.194) | copy-start | bytes 6148
  27.4 11.5 %copy-start.24 = (f32[32,16]{0,1:T(8,128)}, f32[32,16]{0,1:T(8,128)S(1)}, u32[]{:S(2)}) copy-start(f32[32,16]{0,1:T(8,128)S(1)} %copy.196) | copy-start | bytes 6148
  27.5 11.3 %copy-start.18 = (f32[32,16]{0,1:T(8,128)}, f32[32,16]{0,1:T(8,128)S(1)}, u32[]{:S(2)}) copy-start(f32[32,16]{0,1:T(8,128)S(1)} %copy.198) | copy-start | bytes 6148
  27.5 11.2 %copy-start.31 = (f32[32,16]{0,1:T(8,128)}, f32[32,16]{0,1:T(8,128)S(1)}, u32[]{:S(2)}) copy-start(f32[32,16]{0,1:T(8,128)S(1)} %copy.200) | copy-start | bytes 6148
  53.2 13.9 %copy-start.27 = (f32[32,16]{0,1:T(8,128)S(1)}, f32[32,16]{0,1:T(8,128)}, u32[]{:S(2)}) copy-start(f32[32,16]{0,1:T(8,128)} %copy.201) | copy-start | bytes 6148
  53.2 13.9 %copy-start.29 = (f32[32,16]{0,1:T(8,128)S(1)}, f32[32,16]{0,1:T(8,128)}, u32[]{:S(2)}) copy-start(f32[32,16]{0,1:T(8,128)} %copy.188) | copy-start | bytes 6148
  53.3 13.9 %copy-start.40 = (f32[64]{0:T(128)S(1)}, f32[64]{0:T(128)}, u32[]{:S(2)}) copy-start(f32[64]{0:T(128)} %broadcast_subtract_fusion) | copy-start | bytes 772
  68.9 14.2 %copy-start.20 = (bf16[128,1024]{1,0:T(8,128)(2,1)S(1)}, bf16[128,1024]{1,0:T(8,128)(2,1)}, u32[]{:S(2)}) copy-start(bf16[128,1024]{1,0:T(8,128)(2,1)} %param.7) | copy-start | bytes 786436
  72.0 23.0 %all-to-all-start.3 = ((bf16[32,128,32]{1,2,0:T(8,128)(2,1)}), bf16[32,128,32]{1,2,0:T(8,128)(2,1)S(1)}, u32[]{:S(2)}, u32[]{:S(2)}) async-start(bf16[32,128,32]{1,2,0:T(8,128)(2,1)} %copy.211), calls=%async_computation.3 | async-start | bytes 524288 | tf_op jit(solution)/shard_map/all_to_all | solution.py:160
  96.8 15.8 %all-to-all-start = ((bf16[128,32,32]{0,2,1:T(8,128)(2,1)}), bf16[128,32,32]{0,2,1:T(8,128)(2,1)S(1)}, u32[]{:S(2)}, u32[]{:S(2)}) async-start(bf16[128,32,32]{0,2,1:T(8,128)(2,1)} %bitcast), calls=%async_computation | async-start | bytes 524288 | tf_op jit(solution)/shard_map/all_to_all | solution.py:140
  117.8 4.7 copy-start.19
  117.8 4.8 copy-start.32
  119.0 0.7 copy-start.11
  120.4 0.7 copy-start.15
  121.8 3.3 copy-start.16
  121.8 3.9 copy-start.17
  219.5 4.0 copy-start.6
  219.5 4.0 copy-start.7
  224.2 3.9 copy-start.12
  225.6 2.9 copy-start.35
  225.6 14.2 %copy-start.13 = (f32[32,32,16]{1,2,0:T(8,128)S(1)}, f32[32,32,16]{1,2,0:T(8,128)}, u32[]{:S(2)}) copy-start(f32[32,32,16]{1,2,0:T(8,128)} %add.388) | copy-start | bytes 196612
  225.6 14.4 %copy-start.14 = (f32[31,32,16]{1,2,0:T(8,128)S(1)}, f32[31,32,16]{1,2,0:T(8,128)}, u32[]{:S(2)}) copy-start(f32[31,32,16]{1,2,0:T(8,128)} %get-tuple-element.42) | copy-start | bytes 190468
  228.2 22.3 %copy-start = (f32[32,64,64]{2,1,0:T(8,128)S(1)}, f32[32,64,64]{2,1,0:T(8,128)}, u32[]{:S(2)}) copy-start(f32[32,64,64]{2,1,0:T(8,128)} %fusion.77) | copy-start | bytes 1572868
  250.4 4.2 copy-start.9
  250.4 4.3 copy-start.10
  253.9 1.0 copy-start.8
  254.0 1.0 copy-start.28
  254.0 1.0 copy-start.30
  254.0 1.0 copy-start.38
  254.0 1.0 copy-start.39
  254.8 1.3 copy-start.1
  254.8 1.3 copy-start.26
  256.0 8.7 %copy-start.41 = (s32[32]{0:T(128)S(1)}, s32[32]{0:T(128)}, u32[]{:S(2)}) copy-start(s32[32]{0:T(128)} %and_select_fusion) | copy-start | bytes 388
  256.0 9.6 %copy-start.34 = (f32[32,16]{1,0:T(8,128)S(1)}, f32[32,16]{1,0:T(8,128)}, u32[]{:S(2)}) copy-start(f32[32,16]{1,0:T(8,128)} %copy-done.33) | copy-start | bytes 6148
  256.0 19.8 %copy-start.3 = (bf16[128,1024]{0,1:T(8,128)(2,1)S(1)}, bf16[128,1024]{0,1:T(8,128)(2,1)}, u32[]{:S(2)}) copy-start(bf16[128,1024]{0,1:T(8,128)(2,1)} %copy-done.2) | copy-start | bytes 786436
  256.1 19.8 %copy-start.5 = (bf16[128,1024]{0,1:T(8,128)(2,1)S(1)}, bf16[128,1024]{0,1:T(8,128)(2,1)}, u32[]{:S(2)}) copy-start(bf16[128,1024]{0,1:T(8,128)(2,1)} %copy-done.4) | copy-start | bytes 786436
  259.1 16.7 %all-to-all-start.1 = ((bf16[32,128,32]{1,2,0:T(8,128)(2,1)}), bf16[32,128,32]{1,2,0:T(8,128)(2,1)S(1)}, u32[]{:S(2)}, u32[]{:S(2)}) async-start(bf16[32,128,32]{1,2,0:T(8,128)(2,1)} %copy.204), calls=%async_computation.1 | async-start | bytes 524288 | tf_op jit(solution)/shard_map/all_to_all | solution.py:159
  264.0 251.1 %all-reduce.42.cloned.1.call-start = ((), (), s32[]{:S(2)}) async-start(), calls=%async_computation.4 | async-start | bytes 131072 | tf_op jit(solution)/shard_map/psum | solution.py:174
Sparse Core Ops, SparseCore 0:
  271.1 243.9 all-reduce.41
where the time goes:
time: 531 us; the launch traced here: 525 us
  waiting for transfers between devices  264 us (50%)
  local copies, waits for them, and re-layouts  140 us (26%)
  other arithmetic  43.3 us (8%)
  starting transfers between devices  34.4 us (6%)
  matrix products  27.8 us (5%)
  between operations  15 us (3%)
    psum x1, waiting for transfers between devices, per_device(): grad_residues, grad_rates = lax.psum((sum_res, sum_rate), ('ctx', 'tensor'))  237 us
    pad x16, local copies, waits for them, and re-layouts, block_states(): lax.associative_scan(forward_join(rate_c), (span_list, local_out[4], loca...  65.2 us
    unnamed x101, local copies, waits for them, and re-layouts  24.6 us
    all_to_all x1, starting transfers between devices, per_device(): lax.all_to_all(dz_rows, 'ctx', split_axis=1, concat_axis=0, tiled=True)  14.5 us
    slice x2, local copies, waits for them, and re-layouts, apply_states(): after_back = jnp.concatenate([incl_back[1:], zero_row], axis=0)  12.3 us
    add x12, other arithmetic, block_states(): lax.associative_scan(forward_join(rate_c), (span_list, local_out[4], loca...  12.2 us
    concatenate x10, other arithmetic, block_states(): lax.associative_scan(forward_join(rate_c), (span_list, local_out[4], loca...  11.3 us
    all_to_all x1, starting transfers between devices, per_device(): lax.all_to_all(back_send, 'ctx', split_axis=0, concat_axis=1, tiled=True)  11.2 us
  transfers between devices with their start and end apart: 5, of which 5 were waited for; matrix products, arithmetic and copies ran while one was open for 4% of the time, Pallas kernels for 0%

commit v1 on v0

v1 whole, which is shorter than its diff:
```python
import functools

import jax
import jax.numpy as jnp
from jax import lax
from jax.experimental import pallas as pl
from jax.experimental.pallas import tpu as pltpu
from jax.sharding import PartitionSpec as P

MESH = pl.DeviceIdType.MESH
F32 = jnp.float32
BF16 = jnp.bfloat16
EXACT = lax.Precision.HIGHEST

TOK = 128
CHUNKS = 8
PER = 8
GROUP = 16
MODES = 16
PLANE = 16


def iota(shape, dim):
    return lax.broadcasted_iota(jnp.int32, shape, dim)


def dot(a, b, precision=None):
    return lax.dot_general(
        a, b, (((1,), (0,)), ((), ())), precision=precision, preferred_element_type=F32
    )


def dot_nt(a, b):
    return lax.dot_general(a, b, (((1,), (1,)), ((), ())), preferred_element_type=F32)


def kernel(
    q_hbm, k_hbm, v_hbm, g_hbm, res_hbm, rate_hbm,
    op_ref, gq_ref, gk_ref, gv_ref, gres_ref, grate_ref,
    q_v, k_v, v_v, g_v, par, wst, hrev, acoef, rhs, local, lagrev,
    send1, recv1, gsend, grecv, zsend, zrecv, fstate, bstate, send2, recv2, tsend, trecv,
    in_sem, par_sem, send_sem, recv1_sem, recvg_sem, recvz_sem, recv2_sem, recvt_sem,
):
    ctx = lax.axis_index("ctx")
    tau = lax.axis_index("tensor")
    plane = ctx // PLANE
    me = ctx % PLANE
    base = plane * PLANE

    lanes = pl.ds(pl.multiple_of((tau // 2) * 128, 128), 128)
    par_copies = [
        pltpu.make_async_copy(res_hbm.at[:, lanes], par.at[0], par_sem.at[0]),
        pltpu.make_async_copy(rate_hbm.at[:, lanes], par.at[1], par_sem.at[1]),
    ]
    in_copies = [
        pltpu.make_async_copy(src, dst, in_sem.at[i])
        for i, (src, dst) in enumerate(((q_hbm, q_v), (k_hbm, k_v), (g_hbm, g_v), (v_hbm, v_v)))
    ]
    for copy in par_copies + in_copies:
        copy.start()

    barrier = pltpu.get_barrier_semaphore()

    @pl.loop(1, PLANE)
    def _(i):
        pl.semaphore_signal(
            barrier, inc=1, device_id={"ctx": base + (me + i) % PLANE}, device_id_type=MESH
        )

    pl.semaphore_signal(
        barrier, inc=1, device_id={"ctx": (1 - plane) * PLANE + me}, device_id_type=MESH
    )

    @pl.loop(1, 8)
    def _(i):
        pl.semaphore_signal(
            barrier, inc=1, device_id={"tensor": (tau + i) % 8}, device_id_type=MESH
        )

    for copy in par_copies:
        copy.wait()

    lane16 = iota((MODES, 128), 1)
    odd = (tau % 2) == 1

    def own_half(x):
        rolled = pltpu.roll(x, 64, 1)
        first = jnp.where(odd, rolled, x)
        return jnp.where(lane16 < 64, first, jnp.where(odd, x, rolled))

    res_t = own_half(par[0])
    rate_t = own_half(par[1])

    behind = (127 - lane16).astype(F32)
    ahead = (lane16 + 1).astype(F32)

    @pl.loop(0, CHUNKS)
    def _(k):
        shift = (128 - PER * k) % 128
        res_k = pltpu.roll(res_t, shift, 1)
        rate_k = pltpu.roll(rate_t, shift, 1)
        powers = []
        for i in range(PER):
            rate = rate_k[:, i : i + 1]
            res = res_k[:, i : i + 1]
            decay = jnp.exp(-rate * behind)
            wst[k * PER + i, 0:16, :] = decay.astype(BF16)
            wst[k * PER + i, 16:32, :] = (decay * behind).astype(BF16)
            hrev[k, i : i + 1, :] = jnp.sum(res * decay, axis=0, keepdims=True)
            powers.append(res * jnp.exp(-rate * ahead))
        acoef[k] = jnp.concatenate(powers, axis=0).T.astype(BF16)

    for copy in in_copies:
        copy.wait()

    turn = (iota((TOK, TOK), 0) + iota((TOK, TOK), 1) == TOK - 1).astype(BF16)
    group_of = (iota((1, 256), 1) % 128) // GROUP

    @pl.loop(0, CHUNKS)
    def _(k):
        cols = pl.ds(pl.multiple_of(k * 128, 128), 128)
        u = (q_v[:, cols].astype(F32) * k_v[:, cols].astype(F32)).astype(BF16)
        dz = (g_v[:, cols].astype(F32) * v_v[:, cols].astype(F32)).astype(BF16)
        rhs[k, :, 0:128] = u
        rhs[k, :, 128:256] = dot(turn, dz).astype(BF16)
        weights = wst[pl.ds(k * PER, PER)].reshape(PER * 32, TOK)
        ends = dot(weights, rhs[k])
        total = jnp.zeros((32, 256), F32)
        for i in range(PER):
            total = jnp.where(group_of == i, ends[32 * i : 32 * i + 32], total)
        for h in range(2):
            rows = slice(8 * h, 8 * h + 8)
            rows2 = slice(16 + 8 * h, 24 + 8 * h)
            send1[2 * k + h] = jnp.concatenate(
                [
                    total[rows, 0:128],
                    total[rows, 128:256],
                    total[rows2, 0:128],
                    total[rows2, 128:256],
                ],
                axis=0,
            ).astype(BF16)

    pl.semaphore_wait(barrier, PLANE - 1 + 1 + 7)

    @pl.loop(1, PLANE)
    def _(i):
        peer = (me + i) % PLANE
        pltpu.make_async_remote_copy(
            src_ref=send1.at[peer],
            dst_ref=recv1.at[me],
            send_sem=send_sem.at[0],
            recv_sem=recv1_sem,
            device_id={"ctx": base + peer},
            device_id_type=MESH,
        ).start()

    recv1[me] = send1[me]

    row = iota((TOK, TOK), 0)
    lane = iota((TOK, TOK), 1)

    @pl.loop(0, CHUNKS)
    def _(k):
        u = rhs[k, :, 0:128]
        dz = rhs[k, :, 128:256]
        for i in range(PER):
            mine = jnp.where(group_of[:, 0:128] == i, dz, jnp.zeros_like(dz))
            pairs = dot_nt(mine, u)
            diag = pltpu.roll(pairs, 0, 1, stride=1, stride_axis=0)
            lagrev[k, i : i + 1, :] = jnp.sum(
                jnp.where(lane >= row, diag, 0.0), axis=0, keepdims=True
            )

    lag_all = lagrev[...].reshape(64, 128).astype(BF16)
    lag_all = jnp.concatenate([lag_all, lag_all], axis=0)
    lane_filter = iota((32, 128), 1)
    kind_filter = jnp.where(iota((32, 128), 0) < 16, lane_filter, lane_filter - 64)

    def add_filter(k, total):
        part = dot_nt(wst[pl.ds(k * PER, PER)].reshape(PER * 32, TOK), lag_all)
        for i in range(PER):
            total = jnp.where(kind_filter == k * PER + i, part[32 * i : 32 * i + 32], total)
        return total

    local_sums = lax.fori_loop(0, CHUNKS, add_filter, jnp.zeros((32, 128), F32))
    local_sums = local_sums[0:16] + local_sums[16:32]
    gsend[0] = local_sums[0:8]
    gsend[1] = local_sums[8:16]

    @pl.loop(1, PLANE)
    def _(i):
        peer = (me + i) % PLANE
        pltpu.make_async_remote_copy(
            src_ref=gsend.at[peer % 2],
            dst_ref=grecv.at[me],
            send_sem=send_sem.at[1],
            recv_sem=recvg_sem,
            device_id={"ctx": base + peer},
            device_id_type=MESH,
        ).start()

    grecv[me] = gsend[me % 2]

    own_chunk = me // 2
    own_half_id = me % 2
    spread = (iota((128, 128), 0) == PER * own_chunk + iota((128, 128), 1) // GROUP).astype(F32)
    rate_spread = dot(rate_t, spread, EXACT)
    rate_own = jnp.where(own_half_id == 0, rate_spread[0:8], rate_spread[8:16])
    res_own = jnp.where(own_half_id == 0, res_t[0:8], res_t[8:16])
    step = jnp.exp(-rate_own * float(TOK))
    single = jnp.exp(-rate_own)
    collect_lane = iota((128, 128), 1)
    collect_from = PER * own_chunk + iota((128, 128), 0) // GROUP
    collect_one = (collect_lane == collect_from).astype(F32)
    collect_two = (collect_lane == collect_from + 64).astype(F32)

    pltpu.make_async_copy(
        recv1.at[pl.ds(0, PLANE - 1)], recv1.at[pl.ds(0, PLANE - 1)], recv1_sem
    ).wait()

    zero = jnp.zeros((8, 128), F32)
    one, two, sum_one, sum_two = zero, zero, zero, zero
    for m in range(PLANE):
        block = recv1[m].astype(F32)
        end_one, start_one = block[0:8], block[8:16]
        end_two, start_two = block[16:24], block[24:32]
        fstate[m] = one
        sum_one = sum_one + one * start_one
        sum_two = sum_two + two * start_one + one * (start_two + start_one)
        two = step * (two + float(TOK) * one) + end_two
        one = step * one + end_one
    ahead_one, ahead_two = one, two
    one, two = zero, zero
    for m in reversed(range(PLANE)):
        block = recv1[m].astype(F32)
        start_one, start_two = block[8:16], block[24:32]
        bstate[m] = one
        two = step * (two + float(TOK) * one) + start_two
        one = step * one + start_one
    low = plane == 0
    mine_one = jnp.where(low, ahead_one, one)
    mine_two = jnp.where(low, ahead_two, two)

    pltpu.make_async_copy(
        grecv.at[pl.ds(0, PLANE - 1)], grecv.at[pl.ds(0, PLANE - 1)], recvg_sem
    ).wait()
    grads = jnp.sum(grecv[...], axis=0)
    grads = jnp.where((iota((8, 128), 1) % 64) // PER == own_chunk, grads, 0.0)
    grads = grads + dot(single * sum_one, collect_one, EXACT)
    grads = grads + dot(single * sum_two, collect_two, EXACT)
    zsend[0:8] = mine_one
    zsend[8:16] = mine_two
    zsend[16:24] = grads
    z_copy = pltpu.make_async_remote_copy(
        src_ref=zsend,
        dst_ref=zrecv,
        send_sem=send_sem.at[2],
        recv_sem=recvz_sem,
        device_id={"ctx": (1 - plane) * PLANE + me},
        device_id_type=MESH,
    )
    z_copy.start()

    @pl.loop(0, CHUNKS)
    def _(k):
        both = rhs[k]
        total = jnp.zeros((TOK, 256), F32)
        for i in range(PER):
            taps = pltpu.roll(
                jnp.broadcast_to(hrev[k, i : i + 1, :], (TOK, TOK)), 1, 1, stride=1, stride_axis=0
            )
            taps = jnp.where(lane <= row, taps, 0.0).astype(BF16)
            total = jnp.where(group_of == i, dot(taps, both), total)
        local[k] = total

    z_copy.wait_recv()
    other_one, other_two = zrecv[0:8], zrecv[8:16]
    cross_one = single * mine_one * other_one
    cross_two = single * (
        mine_two * other_one + mine_one * other_two + mine_one * other_one
    )
    grads = grads + zrecv[16:24]
    grads = grads + dot(cross_one, collect_one, EXACT) + dot(cross_two, collect_two, EXACT)
    grads = jnp.where(iota((8, 128), 1) < 64, grads, -res_own * grads)
    grads_high = grads.astype(BF16).astype(F32)
    grads_low = grads - grads_high
    into_f = jnp.where(low, 0.0, other_one)
    into_b = jnp.where(low, other_one, 0.0)
    for m in range(PLANE):
        fstate[m] = fstate[m] + into_f
        into_f = step * into_f
    for m in reversed(range(PLANE)):
        send2[m] = jnp.concatenate(
            [fstate[m], bstate[m] + into_b, grads_high, grads_low], axis=0
        ).astype(BF16)
        into_b = step * into_b

    @pl.loop(1, PLANE)
    def _(i):
        peer = (me + i) % PLANE
        pltpu.make_async_remote_copy(
            src_ref=send2.at[peer],
            dst_ref=recv2.at[me],
            send_sem=send_sem.at[3],
            recv_sem=recv2_sem,
            device_id={"ctx": base + peer},
            device_id_type=MESH,
        ).start()

    recv2[me] = send2[me]
    pltpu.make_async_copy(
        recv2.at[pl.ds(0, PLANE - 1)], recv2.at[pl.ds(0, PLANE - 1)], recv2_sem
    ).wait()

    halves = []
    for h in range(2):
        total = jnp.zeros((8, 128), F32)
        for k in range(CHUNKS):
            block = recv2[2 * k + h].astype(F32)
            total = total + (block[16:24] + block[24:32])
        halves.append(total)
    tsend[...] = jnp.concatenate(halves, axis=0)

    @pl.loop(1, 8)
    def _(i):
        pltpu.make_async_remote_copy(
            src_ref=tsend,
            dst_ref=trecv.at[tau],
            send_sem=send_sem.at[4],
            recv_sem=recvt_sem,
            device_id={"tensor": (tau + i) % 8},
            device_id_type=MESH,
        ).start()

    trecv[tau] = tsend[...]

    block_diagonal = (iota((PER, MODES, 256), 2) % 128) // GROUP == iota((PER, MODES, 256), 0)

    @pl.loop(0, CHUNKS)
    def _(k):
        cols = pl.ds(pl.multiple_of(k * 128, 128), 128)
        first = recv2[2 * k].astype(F32)
        second = recv2[2 * k + 1].astype(F32)
        states = jnp.concatenate(
            [
                jnp.concatenate([first[0:8], second[0:8]], axis=0),
                jnp.concatenate([first[8:16], second[8:16]], axis=0),
            ],
            axis=1,
        )
        states = jnp.where(block_diagonal, states[None], 0.0).reshape(PER * MODES, 256)
        total = local[k] + dot(acoef[k], states.astype(BF16))
        conv = total[:, 0:128].astype(BF16).astype(F32)
        back = dot(turn, total[:, 128:256].astype(BF16))
        op_ref[:, cols] = (v_v[:, cols].astype(F32) * conv).astype(BF16)
        gv_ref[:, cols] = (g_v[:, cols].astype(F32) * conv).astype(BF16)
        gq_ref[:, cols] = (k_v[:, cols].astype(F32) * back).astype(BF16)
        gk_ref[:, cols] = (q_v[:, cols].astype(F32) * back).astype(BF16)

    pltpu.make_async_copy(trecv.at[pl.ds(0, 7)], trecv.at[pl.ds(0, 7)], recvt_sem).wait()
    for j in range(4):
        even, uneven = trecv[2 * j], trecv[2 * j + 1]
        gres_ref[:, 128 * j : 128 * j + 128] = jnp.where(
            lane16 < 64, even, pltpu.roll(uneven, 64, 1)
        )
        grate_ref[:, 128 * j : 128 * j + 128] = jnp.where(
            lane16 < 64, pltpu.roll(even, 64, 1), uneven
        )

    def sent(ref, count, sem):
        pltpu.make_async_copy(ref.at[pl.ds(0, count)], ref.at[pl.ds(0, count)], sem).wait()

    sent(send1, PLANE - 1, send_sem.at[0])
    sent(grecv, PLANE - 1, send_sem.at[1])
    z_copy.wait_send()
    sent(send2, PLANE - 1, send_sem.at[3])
    sent(trecv, 7, send_sem.at[4])


def per_device(query_rows, key_rows, value_rows, grad_rows, residues, decay_rates):
    rows, width = query_rows.shape
    any_spec = pl.BlockSpec(memory_space=pl.ANY)
    vmem_spec = pl.BlockSpec(memory_space=pltpu.VMEM)
    wide = jax.ShapeDtypeStruct((rows, width), BF16)
    small = jax.ShapeDtypeStruct((MODES, 512), F32)
    dma = pltpu.SemaphoreType.DMA
    outs = pl.pallas_call(
        kernel,
        out_shape=(wide, wide, wide, wide, small, small),
        in_specs=[any_spec] * 6,
        out_specs=[vmem_spec] * 6,
        scratch_shapes=[
            pltpu.VMEM((rows, width), BF16),
            pltpu.VMEM((rows, width), BF16),
            pltpu.VMEM((rows, width), BF16),
            pltpu.VMEM((rows, width), BF16),
            pltpu.VMEM((2, MODES, 128), F32),
            pltpu.VMEM((64, 32, 128), BF16),
            pltpu.VMEM((CHUNKS, PER, 128), F32),
            pltpu.VMEM((CHUNKS, TOK, 128), BF16),
            pltpu.VMEM((CHUNKS, TOK, 256), BF16),
            pltpu.VMEM((CHUNKS, TOK, 256), F32),
            pltpu.VMEM((CHUNKS, PER, 128), F32),
            pltpu.VMEM((PLANE, 32, 128), BF16),
            pltpu.VMEM((PLANE, 32, 128), BF16),
            pltpu.VMEM((2, 8, 128), F32),
            pltpu.VMEM((PLANE, 8, 128), F32),
            pltpu.VMEM((24, 128), F32),
            pltpu.VMEM((24, 128), F32),
            pltpu.VMEM((PLANE, 8, 128), F32),
            pltpu.VMEM((PLANE, 8, 128), F32),
            pltpu.VMEM((PLANE, 32, 128), BF16),
            pltpu.VMEM((PLANE, 32, 128), BF16),
            pltpu.VMEM((MODES, 128), F32),
            pltpu.VMEM((8, MODES, 128), F32),
            dma((4,)),
            dma((2,)),
            dma((5,)),
            dma(()),
            dma(()),
            dma(()),
            dma(()),
            dma(()),
        ],
        compiler_params=pltpu.CompilerParams(
            collective_id=0, has_side_effects=True, vmem_limit_bytes=32 * 1024 * 1024
        ),
    )(query_rows, key_rows, value_rows, grad_rows, residues.T, decay_rates.T)
    op, gq, gk, gv, gres, grate = outs
    return op, gq, gk, gv, gres.T, grate.T


def solution(mesh):
    wide = P("ctx", "tensor")
    return jax.shard_map(
        per_device,
        mesh=mesh,
        in_specs=(wide, wide, wide, wide, P(), P()),
        out_specs=(wide, wide, wide, wide, P(), P()),
        check_vma=False,
    )
```

time: 531 us -> 46.2 us (0.09); the launches traced: 525 us -> 45.8 us
  waiting for transfers between devices: 264 us -> 0 us
  local copies, waits for them, and re-layouts: 140 us -> 9.35 us
  other arithmetic: 43.3 us -> 0 us
  Pallas kernels: 0 us -> 35.8 us
  starting transfers between devices: 34.4 us -> 0 us
  matrix products: 27.8 us -> 0 us
  between operations: 15 us -> 0.66 us
    psum x1 -> x0, waiting for transfers between devices: 237 us -> none  [per_device(): grad_residues, grad_rates = lax.psum((sum_res, sum_rate), ('ctx', 'tensor'))]
    pad x24 -> x0, local copies, waits for them, and re-layouts: 65.7 us -> none  [the longest x16 65.2 us: block_states(): lax.associative_scan(forward_join(rate_c), (span_list, local_out[4], loca...]
    slice x18 -> x0, local copies, waits for them, and re-layouts: 40 us -> none  [the longest x2 12.3 us: apply_states(): after_back = jnp.concatenate([incl_back[1:], zero_row], axis=0)]
    pallas_call x0 -> x1, Pallas kernels: none -> 35.8 us  [per_device(): pl.pallas_call(kernel, out_shape=(wide, wide, wide, wide, small, small),...]
    all_to_all x4 -> x0, starting transfers between devices: 34.4 us -> none  [the longest x1 14.5 us: per_device(): lax.all_to_all(dz_rows, 'ctx', split_axis=1, concat_axis=0, tiled=True)]
    dot_general x16 -> x0, matrix products: 27.8 us -> none  [the longest x1 7.36 us: local_terms(): toeplitz = jnp.einsum('cj,tsj->cts', kernel, lag_grid, precision=exact_mode)]
    all_to_all x4 -> x0, waiting for transfers between devices: 26.8 us -> none  [the longest x1 9.87 us: per_device(): lax.all_to_all(back_send, 'ctx', split_axis=0, concat_axis=1, tiled=True)]
    add x37 -> x0, other arithmetic: 25.4 us -> none  [the longest x12 12.2 us: block_states(): lax.associative_scan(forward_join(rate_c), (span_list, local_out[4], loca...]
  transfers between devices with their start and end apart: 5 -> 0, of which waited for: 5 -> 0; matrix products, arithmetic and copies ran while one was open for 4% -> 0% of each run, Pallas kernels for 0% -> 0%
where the time goes in v1:
time: 46.2 us; the launch traced here: 45.8 us
  Pallas kernels  35.8 us (77%)
  local copies, waits for them, and re-layouts  9.35 us (20%)
  between operations  0.66 us (1%)
    pallas_call x1, Pallas kernels, per_device(): pl.pallas_call(kernel, out_shape=(wide, wide, wide, wide, small, small),...  35.8 us
    unnamed x18, local copies, waits for them, and re-layouts  9.35 us

profile of v1, /device:TPU:1, one launch (start us, length us, event | category | flops | bytes accessed | tf_op | source)
XLA Modules:
  0.0 45.8 jit_solution(10416547926848164713)
XLA Ops:
  0.6 0.0 copy-start
  0.6 0.9 %copy-done = bf16[128,1024]{1,0:T(8,128)(2,1)S(1)} copy-done((bf16[128,1024]{1,0:T(8,128)(2,1)S(1)}, bf16[128,1024]{1,0:T(8,128)(2,1)}, u32[]{:S(2)}) %copy-start) | copy-done | bytes 262168
  1.6 0.0 copy-start.1
  1.6 0.9 %copy-done.1 = bf16[128,1024]{1,0:T(8,128)(2,1)S(1)} copy-done((bf16[128,1024]{1,0:T(8,128)(2,1)S(1)}, bf16[128,1024]{1,0:T(8,128)(2,1)}, u32[]{:S(2)}) %copy-start.1) | copy-done | bytes 262168
  2.5 0.0 copy-start.2
  2.5 0.9 %copy-done.2 = bf16[128,1024]{1,0:T(8,128)(2,1)S(1)} copy-done((bf16[128,1024]{1,0:T(8,128)(2,1)S(1)}, bf16[128,1024]{1,0:T(8,128)(2,1)}, u32[]{:S(2)}) %copy-start.2) | copy-done | bytes 262168
  3.5 0.0 copy-start.3
  3.5 0.9 %copy-done.3 = bf16[128,1024]{1,0:T(8,128)(2,1)S(1)} copy-done((bf16[128,1024]{1,0:T(8,128)(2,1)S(1)}, bf16[128,1024]{1,0:T(8,128)(2,1)}, u32[]{:S(2)}) %copy-start.3) | copy-done | bytes 262168
  4.4 0.0 copy-start.4
  4.4 0.8 %copy-done.4 = f32[512,16]{0,1:T(8,128)S(1)} copy-done((f32[512,16]{0,1:T(8,128)S(1)}, f32[512,16]{0,1:T(8,128)}, u32[]{:S(2)}) %copy-start.4) | copy-done | bytes 32792
  5.2 0.0 copy-start.5
  5.2 0.8 %copy-done.5 = f32[512,16]{0,1:T(8,128)S(1)} copy-done((f32[512,16]{0,1:T(8,128)S(1)}, f32[512,16]{0,1:T(8,128)}, u32[]{:S(2)}) %copy-start.5) | copy-done | bytes 32792
  6.0 35.8 %shard_map.109 = (bf16[128,1024]{1,0:T(8,128)(2,1)S(1)}, bf16[128,1024]{1,0:T(8,128)(2,1)S(1)}, bf16[128,1024]{1,0:T(8,128)(2,1)S(1)}, bf16[128,1024]{1,0:T(8,12...) custom-call(bf16[128,1024]{1,0:T(8,128)(2,1)S(1)} %copy-done, bf16[128,1024]{1,0:T(8,128)(2,1)S(1)} %copy-done.1, ...), custom_call_target="tpu_custom_call" | custom-call | tf_op jit(solution)/shard_map/pallas_call | solution.py:388
  41.8 0.7 %copy.18 = bf16[128,1024]{1,0:T(8,128)(2,1)} copy(bf16[128,1024]{1,0:T(8,128)(2,1)S(1)} %get-tuple-element.24) | data formatting | bytes 524288
  42.5 0.7 %copy.19 = bf16[128,1024]{1,0:T(8,128)(2,1)} copy(bf16[128,1024]{1,0:T(8,128)(2,1)S(1)} %get-tuple-element.25) | data formatting | bytes 524288
  43.2 0.7 %copy.20 = bf16[128,1024]{1,0:T(8,128)(2,1)} copy(bf16[128,1024]{1,0:T(8,128)(2,1)S(1)} %get-tuple-element.26) | data formatting | bytes 524288
  43.9 0.7 %copy.21 = bf16[128,1024]{1,0:T(8,128)(2,1)} copy(bf16[128,1024]{1,0:T(8,128)(2,1)S(1)} %get-tuple-element.27) | data formatting | bytes 524288
  44.6 0.6 %copy.22 = f32[512,16]{0,1:T(8,128)} copy(f32[512,16]{0,1:T(8,128)S(1)} %bitcast.7) | data formatting | bytes 65536
  45.2 0.6 %copy.23 = f32[512,16]{0,1:T(8,128)} copy(f32[512,16]{0,1:T(8,128)S(1)} %bitcast.6) | data formatting | bytes 65536
Async XLA Ops:
  0.6 1.0 %copy-start = (bf16[128,1024]{1,0:T(8,128)(2,1)S(1)}, bf16[128,1024]{1,0:T(8,128)(2,1)}, u32[]{:S(2)}) copy-start(bf16[128,1024]{1,0:T(8,128)(2,1)} %q_hbm.1) | copy-start | bytes 786436
  1.6 0.9 %copy-start.1 = (bf16[128,1024]{1,0:T(8,128)(2,1)S(1)}, bf16[128,1024]{1,0:T(8,128)(2,1)}, u32[]{:S(2)}) copy-start(bf16[128,1024]{1,0:T(8,128)(2,1)} %k_hbm.1) | copy-start | bytes 786436
  2.5 0.9 %copy-start.2 = (bf16[128,1024]{1,0:T(8,128)(2,1)S(1)}, bf16[128,1024]{1,0:T(8,128)(2,1)}, u32[]{:S(2)}) copy-start(bf16[128,1024]{1,0:T(8,128)(2,1)} %v_hbm.1) | copy-start | bytes 786436
  3.5 0.9 %copy-start.3 = (bf16[128,1024]{1,0:T(8,128)(2,1)S(1)}, bf16[128,1024]{1,0:T(8,128)(2,1)}, u32[]{:S(2)}) copy-start(bf16[128,1024]{1,0:T(8,128)(2,1)} %g_hbm.1) | copy-start | bytes 786436
  4.4 0.8 %copy-start.4 = (f32[512,16]{0,1:T(8,128)S(1)}, f32[512,16]{0,1:T(8,128)}, u32[]{:S(2)}) copy-start(f32[512,16]{0,1:T(8,128)} %param.10) | copy-start | bytes 98308
  5.2 0.8 %copy-start.5 = (f32[512,16]{0,1:T(8,128)S(1)}, f32[512,16]{0,1:T(8,128)}, u32[]{:S(2)}) copy-start(f32[512,16]{0,1:T(8,128)} %param.11) | copy-start | bytes 98308

commit v2 on v1

v2 whole, which is shorter than its diff:
```python
import functools

import jax
import jax.numpy as jnp
from jax import lax
from jax.experimental import pallas as pl
from jax.experimental.pallas import tpu as pltpu
from jax.sharding import PartitionSpec as P

MESH = pl.DeviceIdType.MESH
F32 = jnp.float32
BF16 = jnp.bfloat16
EXACT = lax.Precision.HIGHEST

TOK = 128
CHUNKS = 8
PER = 8
GROUP = 16
MODES = 16
PLANE = 16


def iota(shape, dim):
    return lax.broadcasted_iota(jnp.int32, shape, dim)


def dot(a, b, precision=None):
    return lax.dot_general(
        a, b, (((1,), (0,)), ((), ())), precision=precision, preferred_element_type=F32
    )


def dot_nt(a, b):
    return lax.dot_general(a, b, (((1,), (1,)), ((), ())), preferred_element_type=F32)


def kernel(
    q_hbm, k_hbm, v_hbm, g_hbm, res_hbm, rate_hbm,
    op_hbm, gq_hbm, gk_hbm, gv_hbm, grads_hbm,
    op_ref, gq_ref, gk_ref, gv_ref,
    q_v, k_v, v_v, g_v, par, wst, hrev, acoef, rhs, local, lagrev,
    send1, recv1, across, gsend, grecv, fstate, send2, recv2, xsend, xrecv, ysend,
    in_sem, out_sem, par_sem, send_sem,
    recv1_sem, across_sem, recvg_sem, recv2_sem, recvx_sem, recvy_sem, own_sem,
):
    def arrived(ref, count, sem):
        pltpu.make_async_copy(ref.at[pl.ds(0, count)], ref.at[pl.ds(0, count)], sem).wait()

    ctx = lax.axis_index("ctx")
    tau = lax.axis_index("tensor")
    plane = ctx // PLANE
    me = ctx % PLANE
    base = plane * PLANE
    other = (1 - plane) * PLANE
    column = plane * 8 + tau

    def along_z(i):
        peer = (column + i) % 16
        return {"ctx": (peer // 8) * PLANE + me, "tensor": peer % 8}

    lanes = pl.ds(pl.multiple_of((tau // 2) * 128, 128), 128)
    par_copies = [
        pltpu.make_async_copy(res_hbm.at[:, lanes], par.at[0], par_sem.at[0]),
        pltpu.make_async_copy(rate_hbm.at[:, lanes], par.at[1], par_sem.at[1]),
    ]
    in_copies = [
        pltpu.make_async_copy(src, dst, in_sem.at[i])
        for i, (src, dst) in enumerate(((q_hbm, q_v), (k_hbm, k_v), (g_hbm, g_v), (v_hbm, v_v)))
    ]
    for copy in par_copies + in_copies:
        copy.start()

    barrier = pltpu.get_barrier_semaphore()

    @pl.loop(1, 2 * PLANE)
    def _(i):
        pl.semaphore_signal(
            barrier, inc=1, device_id={"ctx": (ctx + i) % (2 * PLANE)}, device_id_type=MESH
        )

    @pl.loop(1, 16)
    def _(i):
        pl.semaphore_signal(barrier, inc=1, device_id=along_z(i), device_id_type=MESH)

    for copy in par_copies:
        copy.wait()

    lane16 = iota((MODES, 128), 1)
    odd = (tau % 2) == 1

    def own_half(x):
        rolled = pltpu.roll(x, 64, 1)
        first = jnp.where(odd, rolled, x)
        return jnp.where(lane16 < 64, first, jnp.where(odd, x, rolled))

    res_t = own_half(par[0])
    rate_t = own_half(par[1])

    behind = (127 - lane16).astype(F32)
    ahead = (lane16 + 1).astype(F32)

    for k in range(CHUNKS):
        for i in range(PER):
            f = k * PER + i
            decay = jnp.exp(-rate_t[:, f : f + 1] * behind)
            wst[f, 0:16, :] = decay.astype(BF16)
            wst[f, 16:32, :] = (decay * behind).astype(BF16)

    for copy in in_copies:
        copy.wait()

    turn = (iota((TOK, TOK), 0) + iota((TOK, TOK), 1) == TOK - 1).astype(BF16)
    group_of = (iota((1, 256), 1) % 128) // GROUP

    for k in range(CHUNKS):
        cols = slice(128 * k, 128 * k + 128)
        rhs[k, :, 0:128] = (q_v[:, cols].astype(F32) * k_v[:, cols].astype(F32)).astype(BF16)
        dz = (g_v[:, cols].astype(F32) * v_v[:, cols].astype(F32)).astype(BF16)
        rhs[k, :, 128:256] = dot(turn, dz).astype(BF16)

    for k in range(CHUNKS):
        weights = wst[pl.ds(k * PER, PER)].reshape(PER * 32, TOK)
        ends = dot(weights, rhs[k])
        total = jnp.zeros((32, 256), F32)
        for i in range(PER):
            total = jnp.where(group_of == i, ends[32 * i : 32 * i + 32], total)
        for h in range(2):
            rows = slice(8 * h, 8 * h + 8)
            rows2 = slice(16 + 8 * h, 24 + 8 * h)
            send1[2 * k + h] = jnp.concatenate(
                [
                    total[rows, 0:128],
                    total[rows, 128:256],
                    total[rows2, 0:128],
                    total[rows2, 128:256],
                ],
                axis=0,
            ).astype(BF16)

    pl.semaphore_wait(barrier, 2 * PLANE - 1 + 15)

    @pl.loop(0, PLANE)
    def _(i):
        peer = (me + i) % PLANE
        pltpu.make_async_remote_copy(
            src_ref=send1.at[peer, pl.ds(0, 16)],
            dst_ref=across.at[me],
            send_sem=send_sem.at[2],
            recv_sem=across_sem,
            device_id={"ctx": other + peer},
            device_id_type=MESH,
        ).start()


    @pl.loop(1, PLANE)
    def _(i):
        peer = (me + i) % PLANE
        pltpu.make_async_remote_copy(
            src_ref=send1.at[peer],
            dst_ref=recv1.at[me],
            send_sem=send_sem.at[0],
            recv_sem=recv1_sem,
            device_id={"ctx": base + peer},
            device_id_type=MESH,
        ).start()

    recv1[me] = send1[me]

    row = iota((TOK, TOK), 0)
    lane = iota((TOK, TOK), 1)

    @pl.loop(0, CHUNKS, unroll=True)
    def _(k):
        u = rhs[k, :, 0:128]
        dz = rhs[k, :, 128:256]
        for i in range(PER):
            mine = jnp.where(group_of[:, 0:128] == i, dz, jnp.zeros_like(dz))
            pairs = dot_nt(mine, u)
            diag = pltpu.roll(pairs, 0, 1, stride=1, stride_axis=0)
            lagrev[k, i : i + 1, :] = jnp.sum(
                jnp.where(lane >= row, diag, 0.0), axis=0, keepdims=True
            )

    lag_all = lagrev[...].reshape(64, 128).astype(BF16)
    lag_all = jnp.concatenate([lag_all, lag_all], axis=0)
    lane_filter = iota((32, 128), 1)
    kind_filter = jnp.where(iota((32, 128), 0) < 16, lane_filter, lane_filter - 64)

    def add_filter(k, total):
        part = dot_nt(wst[pl.ds(k * PER, PER)].reshape(PER * 32, TOK), lag_all)
        for i in range(PER):
            total = jnp.where(kind_filter == k * PER + i, part[32 * i : 32 * i + 32], total)
        return total

    local_sums = lax.fori_loop(0, CHUNKS, add_filter, jnp.zeros((32, 128), F32), unroll=True)
    local_sums = local_sums[0:16] + local_sums[16:32]
    local_sums = jnp.where(lane16 < 64, local_sums, -res_t * local_sums)
    gsend[0] = local_sums[0:8]
    gsend[1] = local_sums[8:16]

    @pl.loop(1, PLANE)
    def _(i):
        peer = (me + i) % PLANE
        pltpu.make_async_remote_copy(
            src_ref=gsend.at[peer % 2],
            dst_ref=grecv.at[me],
            send_sem=send_sem.at[1],
            recv_sem=recvg_sem,
            device_id={"ctx": base + peer},
            device_id_type=MESH,
        ).start()

    grecv[me] = gsend[me % 2]

    for k in range(CHUNKS):
        powers = []
        for i in range(PER):
            f = k * PER + i
            rate = rate_t[:, f : f + 1]
            res = res_t[:, f : f + 1]
            decay = res * jnp.exp(-rate * behind)
            hrev[k, i : i + 1, :] = jnp.sum(decay, axis=0, keepdims=True)
            powers.append(res * jnp.exp(-rate * ahead))
        acoef[k] = jnp.concatenate(powers, axis=0).T.astype(BF16)

    @pl.loop(0, CHUNKS, unroll=True)
    def _(k):
        both = rhs[k]
        total = jnp.zeros((TOK, 256), F32)
        for i in range(PER):
            taps = pltpu.roll(
                jnp.broadcast_to(hrev[k, i : i + 1, :], (TOK, TOK)), 1, 1, stride=1, stride_axis=0
            )
            taps = jnp.where(lane <= row, taps, 0.0).astype(BF16)
            total = jnp.where(group_of == i, dot(taps, both), total)
        local[k] = total

    own_chunk = me // 2
    upper = (me % 2) == 1
    spread = (iota((128, 128), 0) == PER * own_chunk + iota((128, 128), 1) // GROUP).astype(F32)
    rate_spread = dot(rate_t, spread, EXACT)
    res_spread = dot(res_t, spread, EXACT)
    rate_own = jnp.where(upper, rate_spread[8:16], rate_spread[0:8])
    res_own = jnp.where(upper, res_spread[8:16], res_spread[0:8])
    step = jnp.exp(-rate_own * float(TOK))
    single = jnp.exp(-rate_own)
    collect = (iota((128, 128), 1) % 64 == 8 * tau + iota((128, 128), 0) // GROUP).astype(BF16)
    lane8 = iota((8, 128), 1)
    high = plane == 1

    arrived(recv1, PLANE - 1, recv1_sem)
    arrived(across, PLANE, across_sem)

    zero = jnp.zeros((8, 128), F32)
    incoming = zero
    for i in range(PLANE):
        block = across[jnp.where(high, i, PLANE - 1 - i)].astype(F32)
        incoming = step * incoming + jnp.where(high, block[0:8], block[8:16])
    forward = jnp.where(high, incoming, 0.0)
    backward = jnp.where(high, 0.0, incoming)
    for m in range(PLANE):
        fstate[m] = forward
        forward = step * forward + recv1[m, 0:16, :].astype(F32)[0:8]
    sum_one, sum_two, sum_mid = zero, zero, zero
    for m in reversed(range(PLANE)):
        block = recv1[m].astype(F32)
        start_one, end_two, start_two = block[8:16], block[16:24], block[24:32]
        forward = fstate[m]
        send2[m] = jnp.concatenate([forward, backward], axis=0).astype(BF16)
        sum_one = sum_one + forward * start_one
        sum_two = sum_two + (forward * start_two + end_two * backward)
        sum_mid = sum_mid + forward * backward
        backward = step * backward + start_one

    @pl.loop(1, PLANE)
    def _(i):
        peer = (me + i) % PLANE
        pltpu.make_async_remote_copy(
            src_ref=send2.at[peer],
            dst_ref=recv2.at[me],
            send_sem=send_sem.at[3],
            recv_sem=recv2_sem,
            device_id={"ctx": base + peer},
            device_id_type=MESH,
        ).start()

    sum_two = -res_own * single * (sum_two + sum_one + float(TOK) * step * sum_mid)
    sum_one = single * sum_one
    one_high, two_high = sum_one.astype(BF16), sum_two.astype(BF16)
    parts = jnp.concatenate(
        [
            one_high.astype(F32),
            sum_one - one_high.astype(F32),
            two_high.astype(F32),
            sum_two - two_high.astype(F32),
        ],
        axis=0,
    ).astype(BF16)
    parts = dot(parts, collect)
    grads = jnp.where(lane8 < 64, parts[0:8] + parts[8:16], parts[16:24] + parts[24:32])
    arrived(grecv, PLANE - 1, recvg_sem)
    inside = jnp.where((lane8 % 64) // PER == own_chunk, jnp.sum(grecv[...], axis=0), 0.0)
    grads = grads + pltpu.roll(inside, (128 + PER * (tau - own_chunk)) % 128, 1)
    xsend[...] = grads

    @pl.loop(1, 16)
    def _(i):
        pltpu.make_async_remote_copy(
            src_ref=xsend,
            dst_ref=xrecv.at[column],
            send_sem=send_sem.at[4],
            recv_sem=recvx_sem,
            device_id=along_z(i),
            device_id_type=MESH,
        ).start()

    xrecv[column] = grads
    recv2[me] = send2[me]

    arrived(xrecv, 15, recvx_sem)
    ysend[...] = jnp.sum(xrecv[...], axis=0)

    @pl.loop(1, PLANE)
    def _(i):
        pltpu.make_async_remote_copy(
            src_ref=ysend,
            dst_ref=grads_hbm.at[me],
            send_sem=send_sem.at[5],
            recv_sem=recvy_sem,
            device_id={"ctx": base + (me + i) % PLANE},
            device_id_type=MESH,
        ).start()

    own_copy = pltpu.make_async_copy(ysend, grads_hbm.at[me], own_sem)
    own_copy.start()

    arrived(recv2, PLANE - 1, recv2_sem)

    block_diagonal = (iota((PER, MODES, 256), 2) % 128) // GROUP == iota((PER, MODES, 256), 0)

    @pl.loop(0, CHUNKS, unroll=True)
    def _(k):
        cols = pl.ds(pl.multiple_of(k * 128, 128), 128)
        first = recv2[2 * k].astype(F32)
        second = recv2[2 * k + 1].astype(F32)
        states = jnp.concatenate(
            [
                jnp.concatenate([first[0:8], second[0:8]], axis=0),
                jnp.concatenate([first[8:16], second[8:16]], axis=0),
            ],
            axis=1,
        )
        states = jnp.where(block_diagonal, states[None], 0.0).reshape(PER * MODES, 256)
        total = local[k] + dot(acoef[k], states.astype(BF16))
        conv = total[:, 0:128].astype(BF16).astype(F32)
        back = dot(turn, total[:, 128:256].astype(BF16))
        op_ref[:, cols] = (v_v[:, cols].astype(F32) * conv).astype(BF16)
        gv_ref[:, cols] = (g_v[:, cols].astype(F32) * conv).astype(BF16)
        gq_ref[:, cols] = (k_v[:, cols].astype(F32) * back).astype(BF16)
        gk_ref[:, cols] = (q_v[:, cols].astype(F32) * back).astype(BF16)

    out_copies = [
        pltpu.make_async_copy(src, dst, out_sem.at[i])
        for i, (src, dst) in enumerate(
            ((op_ref, op_hbm), (gq_ref, gq_hbm), (gk_ref, gk_hbm), (gv_ref, gv_hbm))
        )
    ]
    for copy in out_copies:
        copy.start()

    arrived(send1, PLANE - 1, send_sem.at[0])
    arrived(grecv, PLANE - 1, send_sem.at[1])
    arrived(across, PLANE, send_sem.at[2])
    arrived(send2, PLANE - 1, send_sem.at[3])
    arrived(xrecv, 15, send_sem.at[4])
    arrived(xrecv, PLANE - 1, send_sem.at[5])
    own_copy.wait()
    for copy in out_copies:
        copy.wait()
    arrived(grads_hbm, PLANE - 1, recvy_sem)


def hand_over(
    op_in, gq_in, gk_in, gv_in, grads_in,
    op_out, gq_out, gk_out, gv_out, gres_ref, grate_ref,
    op_v, gq_v, gk_v, gv_v, grads_v, into_sem, out_sem,
):
    inputs = (op_in, gq_in, gk_in, gv_in)
    held = (op_v, gq_v, gk_v, gv_v)
    results = (op_out, gq_out, gk_out, gv_out)
    grads_copy = pltpu.make_async_copy(grads_in, grads_v, into_sem.at[4])
    into = [pltpu.make_async_copy(inputs[i], held[i], into_sem.at[i]) for i in range(4)]
    out = [pltpu.make_async_copy(held[i], results[i], out_sem.at[i]) for i in range(4)]
    grads_copy.start()
    for copy in into:
        copy.start()
    grads_copy.wait()

    lane = iota((MODES, 128), 1)
    rows = [
        jnp.concatenate([grads_v[2 * k], grads_v[2 * k + 1]], axis=0) for k in range(CHUNKS)
    ]
    for bit in (4, 2, 1):
        clear = (lane // PER) % (2 * bit) < bit
        turned = list(rows)
        for k in range(CHUNKS):
            if k & bit:
                continue
            near, far = rows[k], rows[k + bit]
            turned[k] = jnp.where(clear, near, pltpu.roll(far, PER * bit, 1))
            turned[k + bit] = jnp.where(clear, pltpu.roll(near, 128 - PER * bit, 1), far)
        rows = turned
    for j in range(4):
        even, uneven = rows[2 * j], rows[2 * j + 1]
        gres_ref[:, 128 * j : 128 * j + 128] = jnp.where(
            lane < 64, even, pltpu.roll(uneven, 64, 1)
        )
        grate_ref[:, 128 * j : 128 * j + 128] = jnp.where(
            lane < 64, pltpu.roll(even, 64, 1), uneven
        )

    for i in range(4):
        into[i].wait()
        out[i].start()
    for copy in out:
        copy.wait()


def per_device(query_rows, key_rows, value_rows, grad_rows, residues, decay_rates):
    rows, width = query_rows.shape
    any_spec = pl.BlockSpec(memory_space=pl.ANY)
    vmem_limit = 60 * 1024 * 1024
    wide = jax.ShapeDtypeStruct((rows, width), BF16)
    small = jax.ShapeDtypeStruct((MODES, 512), F32)
    dma = pltpu.SemaphoreType.DMA
    whole = pltpu.VMEM((rows, width), BF16)
    outs = pl.pallas_call(
        kernel,
        out_shape=(wide, wide, wide, wide, jax.ShapeDtypeStruct((PLANE, 8, 128), F32)),
        in_specs=[any_spec] * 6,
        out_specs=[any_spec] * 5,
        scratch_shapes=[whole] * 8
        + [
            pltpu.VMEM((2, MODES, 128), F32),
            pltpu.VMEM((64, 32, 128), BF16),
            pltpu.VMEM((CHUNKS, PER, 128), F32),
            pltpu.VMEM((CHUNKS, TOK, 128), BF16),
            pltpu.VMEM((CHUNKS, TOK, 256), BF16),
            pltpu.VMEM((CHUNKS, TOK, 256), F32),
            pltpu.VMEM((CHUNKS, PER, 128), F32),
            pltpu.VMEM((PLANE, 32, 128), BF16),
            pltpu.VMEM((PLANE, 32, 128), BF16),
            pltpu.VMEM((PLANE, 16, 128), BF16),
            pltpu.VMEM((2, 8, 128), F32),
            pltpu.VMEM((PLANE, 8, 128), F32),
            pltpu.VMEM((PLANE, 8, 128), F32),
            pltpu.VMEM((PLANE, 16, 128), BF16),
            pltpu.VMEM((PLANE, 16, 128), BF16),
            pltpu.VMEM((8, 128), F32),
            pltpu.VMEM((16, 8, 128), F32),
            pltpu.VMEM((8, 128), F32),
            dma((4,)),
            dma((4,)),
            dma((2,)),
            dma((6,)),
        ]
        + [dma(())] * 7,
        compiler_params=pltpu.CompilerParams(
            collective_id=0, has_side_effects=True, vmem_limit_bytes=vmem_limit
        ),
    )(query_rows, key_rows, value_rows, grad_rows, residues.T, decay_rates.T)
    vmem_spec = pl.BlockSpec(memory_space=pltpu.VMEM)
    op, gq, gk, gv, gres, grate = pl.pallas_call(
        hand_over,
        out_shape=(wide, wide, wide, wide, small, small),
        in_specs=[any_spec] * 5,
        out_specs=[any_spec] * 4 + [vmem_spec] * 2,
        scratch_shapes=[whole] * 4 + [pltpu.VMEM((PLANE, 8, 128), F32), dma((5,)), dma((4,))],
        compiler_params=pltpu.CompilerParams(vmem_limit_bytes=vmem_limit),
    )(*outs)
    return op, gq, gk, gv, gres.T, grate.T


def solution(mesh):
    wide = P("ctx", "tensor")
    return jax.shard_map(
        per_device,
        mesh=mesh,
        in_specs=(wide, wide, wide, wide, P(), P()),
        out_specs=(wide, wide, wide, wide, P(), P()),
        check_vma=False,
    )
```

time: 46.2 us -> 35 us (0.76)
  local copies, waits for them, and re-layouts: 9.35 us -> 0 us
  Pallas kernels: 35.8 us -> 34.2 us
    unnamed x18 -> x0, local copies, waits for them, and re-layouts: 9.35 us -> none
    pallas_call x1 -> x2, Pallas kernels: 35.8 us -> 34.2 us  [the longest x1 31.4 us: per_device(): pl.pallas_call(kernel, out_shape=(wide, wide, wide, wide, jax.ShapeDtypeS...]
where the time goes in v2:
time: 35 us; the launch traced here: 34.8 us
  Pallas kernels  34.2 us (98%)
  between operations  0.64 us (2%)
    pallas_call x1, Pallas kernels, per_device(): pl.pallas_call(kernel, out_shape=(wide, wide, wide, wide, jax.ShapeDtypeS...  31.4 us
    pallas_call x1, Pallas kernels, per_device(): pl.pallas_call(hand_over, out_shape=(wide, wide, wide, wide, small, small...  2.81 us

profile of v2, /device:TPU:1, one launch (start us, length us, event | category | flops | bytes accessed | tf_op | source)
XLA Modules:
  0.0 34.8 jit_solution(800788151861402722)
XLA Ops:
  0.6 31.4 %shard_map.109 = (bf16[128,1024]{1,0:T(8,128)(2,1)}, bf16[128,1024]{1,0:T(8,128)(2,1)}, bf16[128,1024]{1,0:T(8,128)(2,1)}, bf16[128,1024]{1,0:T(8,128)(2,1)}, f32[16,8,128]{2,1,0:T(8,128)}) custom-call(bf16[128,1024]{1,0:T(8,128)(2,1)} %q_hbm.1, bf16[128,1024]{1,0:T(8,128)(2,1)} %k_hbm.1, bf16[128,1024]{1,0:T(8,128)(2,1)} %v_hbm.1, bf16[128,1024]{1,0:T(8,128)(2,1)} %g_hbm.1, ...), custom_call_target="tpu_custom_call" | custom-call | tf_op jit(solution)/shard_map/pallas_call | solution.py:437
  32.0 2.8 %shard_map.110 = (bf16[128,1024]{1,0:T(8,128)(2,1)}, bf16[128,1024]{1,0:T(8,128)(2,1)}, bf16[128,1024]{1,0:T(8,128)(2,1)}, bf16[128,1024]{1,0:T(8,128)(2,1)}, f32[16,512]{1,0:T(8,128)}, /*index=5*/f32[16,512]{1,0:T(8,128)}) custom-call(bf16[128,1024]{1,0:T(8,128)(2,1)} %get-tuple-element.17.op_in, bf16[128,1024]{1,0:T(8,128)(2,1)} %get-tuple-element.18.gq_in, ...), custom_call_target="tpu_custom_call" | custom-call | tf_op jit(solution)/shard_map/pallas_call | solution.py:473

commit v3 on v2

--- a/solution.py
+++ b/solution.py
@@ -18,6 +18,10 @@
 GROUP = 16
 MODES = 16
 PLANE = 16
+FAR_FIRST = sorted(
+    ((dx, dy) for dx in range(4) for dy in range(4) if dx or dy),
+    key=lambda way: -(min(way[0], 4 - way[0]) + min(way[1], 4 - way[1])),
+)
 
 
 def iota(shape, dim):
@@ -36,27 +40,44 @@
 
 def kernel(
     q_hbm, k_hbm, v_hbm, g_hbm, res_hbm, rate_hbm,
-    op_hbm, gq_hbm, gk_hbm, gv_hbm, grads_hbm,
-    op_ref, gq_ref, gk_ref, gv_ref,
+    op_ref, gq_ref, gk_ref, gv_ref, grads_ref,
     q_v, k_v, v_v, g_v, par, wst, hrev, acoef, rhs, local, lagrev,
-    send1, recv1, across, gsend, grecv, fstate, send2, recv2, xsend, xrecv, ysend,
-    in_sem, out_sem, par_sem, send_sem,
-    recv1_sem, across_sem, recvg_sem, recv2_sem, recvx_sem, recvy_sem, own_sem,
+    send1, recv1, gsend, grecv, tstate, ostate, zsend, zrecv, cross,
+    send2, recv2, xsend, xrecv, ysend,
+    in_sem, par_sem, send_sem,
+    recv1_sem, recvg_sem, recvz_sem, recv2_sem, recvx_sem, recvy_sem, ready_sem,
 ):
-    def arrived(ref, count, sem):
-        pltpu.make_async_copy(ref.at[pl.ds(0, count)], ref.at[pl.ds(0, count)], sem).wait()
-
     ctx = lax.axis_index("ctx")
     tau = lax.axis_index("tensor")
     plane = ctx // PLANE
     me = ctx % PLANE
+    z = plane * 4 + tau // 2
+    core = tau % 2
     base = plane * PLANE
-    other = (1 - plane) * PLANE
-    column = plane * 8 + tau
-
-    def along_z(i):
-        peer = (column + i) % 16
-        return {"ctx": (peer // 8) * PLANE + me, "tensor": peer % 8}
+    first = plane == 0
+    second = plane == 1
+
+    def arrived(ref, count, sem):
+        pltpu.make_async_copy(ref.at[pl.ds(0, count)], ref.at[pl.ds(0, count)], sem).wait()
+
+    def in_plane(offset):
+        return base + ((me // 4 + offset[0]) % 4) * 4 + (me % 4 + offset[1]) % 4
+
+    def send(src, dst, kind, recv_sem, device):
+        pltpu.make_async_remote_copy(
+            src_ref=src,
+            dst_ref=dst,
+            send_sem=send_sem.at[kind],
+            recv_sem=recv_sem,
+            device_id=device,
+            device_id_type=MESH,
+        ).start()
+
+    def z_arrived():
+        pltpu.make_async_copy(zrecv, zrecv, recvz_sem).wait()
+
+    def signal(device):
+        pl.semaphore_signal(barrier, inc=1, device_id=device, device_id_type=MESH)
 
     lanes = pl.ds(pl.multiple_of((tau // 2) * 128, 128), 128)
     par_copies = [
@@ -72,15 +93,19 @@
 
     barrier = pltpu.get_barrier_semaphore()
 
-    @pl.loop(1, 2 * PLANE)
+    @pl.loop(1, PLANE)
     def _(i):
-        pl.semaphore_signal(
-            barrier, inc=1, device_id={"ctx": (ctx + i) % (2 * PLANE)}, device_id_type=MESH
-        )
-
-    @pl.loop(1, 16)
+        signal({"ctx": base + (me + i) % PLANE})
+
+    @pl.loop(1, 8)
     def _(i):
-        pl.semaphore_signal(barrier, inc=1, device_id=along_z(i), device_id_type=MESH)
+        signal({"tensor": (tau + i) % 8})
+
+    @pl.when(first)
+    def _():
+        @pl.loop(0, 8)
+        def _(i):
+            signal({"ctx": PLANE + me, "tensor": (tau + i) % 8})
 
     for copy in par_copies:
         copy.wait()
@@ -137,33 +162,26 @@
                 axis=0,
             ).astype(BF16)
 
-    pl.semaphore_wait(barrier, 2 * PLANE - 1 + 15)
-
-    @pl.loop(0, PLANE)
-    def _(i):
-        peer = (me + i) % PLANE
-        pltpu.make_async_remote_copy(
-            src_ref=send1.at[peer, pl.ds(0, 16)],
-            dst_ref=across.at[me],
-            send_sem=send_sem.at[2],
-            recv_sem=across_sem,
-            device_id={"ctx": other + peer},
-            device_id_type=MESH,
-        ).start()
-
-
-    @pl.loop(1, PLANE)
-    def _(i):
-        peer = (me + i) % PLANE
-        pltpu.make_async_remote_copy(
-            src_ref=send1.at[peer],
-            dst_ref=recv1.at[me],
-            send_sem=send_sem.at[0],
-            recv_sem=recv1_sem,
-            device_id={"ctx": base + peer},
-            device_id_type=MESH,
-        ).start()
-
+    @pl.when(first)
+    def _():
+        pl.semaphore_wait(barrier, PLANE - 1 + 7)
+
+    @pl.when(second)
+    def _():
+        pl.semaphore_wait(barrier, PLANE - 1 + 7 + 8)
+
+        @pl.loop(0, 8)
+        def _(i):
+            pl.semaphore_signal(
+                ready_sem,
+                inc=1,
+                device_id={"ctx": me, "tensor": (tau + i) % 8},
+                device_id_type=MESH,
+            )
+
+    for offset in FAR_FIRST:
+        peer = in_plane(offset)
+        send(send1.at[peer - base], recv1.at[me], 0, recv1_sem, {"ctx": peer})
     recv1[me] = send1[me]
 
     row = iota((TOK, TOK), 0)
@@ -198,18 +216,9 @@
     gsend[0] = local_sums[0:8]
     gsend[1] = local_sums[8:16]
 
-    @pl.loop(1, PLANE)
-    def _(i):
-        peer = (me + i) % PLANE
-        pltpu.make_async_remote_copy(
-            src_ref=gsend.at[peer % 2],
-            dst_ref=grecv.at[me],
-            send_sem=send_sem.at[1],
-            recv_sem=recvg_sem,
-            device_id={"ctx": base + peer},
-            device_id_type=MESH,
-        ).start()
-
+    for offset in FAR_FIRST:
+        peer = in_plane(offset)
+        send(gsend.at[peer % 2], grecv.at[me], 1, recvg_sem, {"ctx": peer})
     grecv[me] = gsend[me % 2]
 
     for k in range(CHUNKS):
@@ -246,46 +255,55 @@
     single = jnp.exp(-rate_own)
     collect = (iota((128, 128), 1) % 64 == 8 * tau + iota((128, 128), 0) // GROUP).astype(BF16)
     lane8 = iota((8, 128), 1)
-    high = plane == 1
+    zero = jnp.zeros((8, 128), F32)
 
     arrived(recv1, PLANE - 1, recv1_sem)
-    arrived(across, PLANE, across_sem)
-
-    zero = jnp.zeros((8, 128), F32)
-    incoming = zero
+
+    def place(i):
+        return jnp.where(first, i, PLANE - 1 - i)
+
+    away_ends = []
+    one, two, sum_one, sum_two = zero, zero, zero, zero
     for i in range(PLANE):
-        block = across[jnp.where(high, i, PLANE - 1 - i)].astype(F32)
-        incoming = step * incoming + jnp.where(high, block[0:8], block[8:16])
-    forward = jnp.where(high, incoming, 0.0)
-    backward = jnp.where(high, 0.0, incoming)
-    for m in range(PLANE):
-        fstate[m] = forward
-        forward = step * forward + recv1[m, 0:16, :].astype(F32)[0:8]
-    sum_one, sum_two, sum_mid = zero, zero, zero
-    for m in reversed(range(PLANE)):
-        block = recv1[m].astype(F32)
-        start_one, end_two, start_two = block[8:16], block[16:24], block[24:32]
-        forward = fstate[m]
-        send2[m] = jnp.concatenate([forward, backward], axis=0).astype(BF16)
-        sum_one = sum_one + forward * start_one
-        sum_two = sum_two + (forward * start_two + end_two * backward)
-        sum_mid = sum_mid + forward * backward
-        backward = step * backward + start_one
-
-    @pl.loop(1, PLANE)
-    def _(i):
-        peer = (me + i) % PLANE
-        pltpu.make_async_remote_copy(
-            src_ref=send2.at[peer],
-            dst_ref=recv2.at[me],
-            send_sem=send_sem.at[3],
-            recv_sem=recv2_sem,
-            device_id={"ctx": base + peer},
-            device_id_type=MESH,
-        ).start()
-
-    sum_two = -res_own * single * (sum_two + sum_one + float(TOK) * step * sum_mid)
-    sum_one = single * sum_one
+        block = recv1[place(i)].astype(F32)
+        toward_one = jnp.where(first, block[0:8], block[8:16])
+        away_one = jnp.where(first, block[8:16], block[0:8])
+        toward_two = jnp.where(first, block[16:24], block[24:32])
+        away_two = jnp.where(first, block[24:32], block[16:24])
+        away_ends.append(away_one)
+        tstate[i] = one
+        sum_one = sum_one + one * away_one
+        sum_two = sum_two + (two * away_one + one * (away_two + away_one))
+        two = step * (two + float(TOK) * one) + toward_two
+        one = step * one + toward_one
+    zsend[0:8] = one
+    zsend[8:16] = two
+    partner = {"ctx": (1 - plane) * PLANE + me}
+
+    @pl.when(first)
+    def _():
+        pl.semaphore_wait(ready_sem, 8)
+
+    send(zsend, zrecv, 3, recvz_sem, partner)
+
+    away = zero
+    for i in reversed(range(PLANE)):
+        ostate[i] = away
+        away = step * away + away_ends[i]
+
+    @pl.when(first)
+    def _():
+        cross[...] = jnp.zeros((16, 128), F32)
+
+    @pl.when(second)
+    def _():
+        z_arrived()
+        other_one, other_two = zrecv[0:8], zrecv[8:16]
+        cross[0:8] = one * other_one
+        cross[8:16] = two * other_one + one * (other_two + other_one)
+
+    sum_one = single * (sum_one + cross[0:8])
+    sum_two = -res_own * single * (sum_two + cross[8:16])
     one_high, two_high = sum_one.astype(BF16), sum_two.astype(BF16)
     parts = jnp.concatenate(
         [
@@ -302,37 +320,36 @@
     inside = jnp.where((lane8 % 64) // PER == own_chunk, jnp.sum(grecv[...], axis=0), 0.0)
     grads = grads + pltpu.roll(inside, (128 + PER * (tau - own_chunk)) % 128, 1)
     xsend[...] = grads
-
-    @pl.loop(1, 16)
-    def _(i):
-        pltpu.make_async_remote_copy(
-            src_ref=xsend,
-            dst_ref=xrecv.at[column],
-            send_sem=send_sem.at[4],
-            recv_sem=recvx_sem,
-            device_id=along_z(i),
-            device_id_type=MESH,
-        ).start()
-
-    xrecv[column] = grads
+    xrecv[plane * 8 + tau] = grads
+
+    for hop in (4, 3, 5, 2, 6, 1, 7, 0):
+        there = (z + hop) % 8
+        for other in (1 - core, core) if hop else (1 - core,):
+            device = {"ctx": (there // 4) * PLANE + me, "tensor": (there % 4) * 2 + other}
+            send(xsend, xrecv.at[plane * 8 + tau], 4, recvx_sem, device)
+
+    @pl.when(first)
+    def _():
+        z_arrived()
+
+    passed = zrecv[0:8]
+    for i in reversed(range(PLANE)):
+        away = ostate[i] + passed
+        send2[place(i)] = jnp.concatenate(
+            [jnp.where(first, tstate[i], away), jnp.where(first, away, tstate[i])], axis=0
+        ).astype(BF16)
+        passed = step * passed
+    for offset in FAR_FIRST:
+        peer = in_plane(offset)
+        send(send2.at[peer - base], recv2.at[me], 2, recv2_sem, {"ctx": peer})
     recv2[me] = send2[me]
 
     arrived(xrecv, 15, recvx_sem)
-    ysend[...] = jnp.sum(xrecv[...], axis=0)
-
-    @pl.loop(1, PLANE)
-    def _(i):
-        pltpu.make_async_remote_copy(
-            src_ref=ysend,
-            dst_ref=grads_hbm.at[me],
-            send_sem=send_sem.at[5],
-            recv_sem=recvy_sem,
-            device_id={"ctx": base + (me + i) % PLANE},
-            device_id_type=MESH,
-        ).start()
-
-    own_copy = pltpu.make_async_copy(ysend, grads_hbm.at[me], own_sem)
-    own_copy.start()
+    total = jnp.sum(xrecv[...], axis=0)
+    ysend[...] = total
+    for offset in FAR_FIRST:
+        send(ysend, grads_ref.at[me], 5, recvy_sem, {"ctx": in_plane(offset)})
+    grads_ref[me] = total
 
     arrived(recv2, PLANE - 1, recv2_sem)
 
@@ -359,42 +376,25 @@
         gq_ref[:, cols] = (k_v[:, cols].astype(F32) * back).astype(BF16)
         gk_ref[:, cols] = (q_v[:, cols].astype(F32) * back).astype(BF16)
 
-    out_copies = [
-        pltpu.make_async_copy(src, dst, out_sem.at[i])
-        for i, (src, dst) in enumerate(
-            ((op_ref, op_hbm), (gq_ref, gq_hbm), (gk_ref, gk_hbm), (gv_ref, gv_hbm))
-        )
-    ]
-    for copy in out_copies:
-        copy.start()
-
     arrived(send1, PLANE - 1, send_sem.at[0])
     arrived(grecv, PLANE - 1, send_sem.at[1])
-    arrived(across, PLANE, send_sem.at[2])
-    arrived(send2, PLANE - 1, send_sem.at[3])
+    arrived(send2, PLANE - 1, send_sem.at[2])
+    pltpu.make_async_copy(zsend, zsend, send_sem.at[3]).wait()
     arrived(xrecv, 15, send_sem.at[4])
-    arrived(xrecv, PLANE - 1, send_sem.at[5])
-    own_copy.wait()
-    for copy in out_copies:
-        copy.wait()
-    arrived(grads_hbm, PLANE - 1, recvy_sem)
+    arrived(grads_ref, PLANE - 1, send_sem.at[5])
+    arrived(grads_ref, PLANE - 1, recvy_sem)
 
 
 def hand_over(
-    op_in, gq_in, gk_in, gv_in, grads_in,
-    op_out, gq_out, gk_out, gv_out, gres_ref, grate_ref,
-    op_v, gq_v, gk_v, gv_v, grads_v, into_sem, out_sem,
+    op_v, gq_v, gk_v, gv_v, grads_v,
+    op_out, gq_out, gk_out, gv_out, gres_out, grate_out,
+    gres_v, grate_v, out_sem,
 ):
-    inputs = (op_in, gq_in, gk_in, gv_in)
-    held = (op_v, gq_v, gk_v, gv_v)
-    results = (op_out, gq_out, gk_out, gv_out)
-    grads_copy = pltpu.make_async_copy(grads_in, grads_v, into_sem.at[4])
-    into = [pltpu.make_async_copy(inputs[i], held[i], into_sem.at[i]) for i in range(4)]
-    out = [pltpu.make_async_copy(held[i], results[i], out_sem.at[i]) for i in range(4)]
-    grads_copy.start()
-    for copy in into:
+    held = (op_v, gq_v, gk_v, gv_v, gres_v, grate_v)
+    results = (op_out, gq_out, gk_out, gv_out, gres_out, grate_out)
+    out = [pltpu.make_async_copy(held[i], results[i], out_sem.at[i]) for i in range(6)]
+    for copy in out[:4]:
         copy.start()
-    grads_copy.wait()
 
     lane = iota((MODES, 128), 1)
     rows = [
@@ -412,16 +412,15 @@
         rows = turned
     for j in range(4):
         even, uneven = rows[2 * j], rows[2 * j + 1]
-        gres_ref[:, 128 * j : 128 * j + 128] = jnp.where(
+        gres_v[:, 128 * j : 128 * j + 128] = jnp.where(
             lane < 64, even, pltpu.roll(uneven, 64, 1)
         )
-        grate_ref[:, 128 * j : 128 * j + 128] = jnp.where(
+        grate_v[:, 128 * j : 128 * j + 128] = jnp.where(
             lane < 64, pltpu.roll(even, 64, 1), uneven
         )
-
-    for i in range(4):
-        into[i].wait()
-        out[i].start()
+    out[4].start()
+    out[5].start()
+
     for copy in out:
         copy.wait()
 
@@ -429,17 +428,18 @@
 def per_device(query_rows, key_rows, value_rows, grad_rows, residues, decay_rates):
     rows, width = query_rows.shape
     any_spec = pl.BlockSpec(memory_space=pl.ANY)
-    vmem_limit = 60 * 1024 * 1024
+    vmem_spec = pl.BlockSpec(memory_space=pltpu.VMEM)
+    vmem_limit = 16 * 1024 * 1024
     wide = jax.ShapeDtypeStruct((rows, width), BF16)
     small = jax.ShapeDtypeStruct((MODES, 512), F32)
     dma = pltpu.SemaphoreType.DMA
     whole = pltpu.VMEM((rows, width), BF16)
     outs = pl.pallas_call(
         kernel,
-        out_shape=(wide, wide, wide, wide, jax.ShapeDtypeStruct((PLANE, 8, 128), F32)),
+        out_shape=(whole, whole, whole, whole, pltpu.VMEM((PLANE, 8, 128), F32)),
         in_specs=[any_spec] * 6,
-        out_specs=[any_spec] * 5,
-        scratch_shapes=[whole] * 8
+        out_specs=[vmem_spec] * 5,
+        scratch_shapes=[whole] * 4
         + [
             pltpu.VMEM((2, MODES, 128), F32),
             pltpu.VMEM((64, 32, 128), BF16),
@@ -450,32 +450,39 @@
             pltpu.VMEM((CHUNKS, PER, 128), F32),
             pltpu.VMEM((PLANE, 32, 128), BF16),
             pltpu.VMEM((PLANE, 32, 128), BF16),
-            pltpu.VMEM((PLANE, 16, 128), BF16),
             pltpu.VMEM((2, 8, 128), F32),
             pltpu.VMEM((PLANE, 8, 128), F32),
             pltpu.VMEM((PLANE, 8, 128), F32),
+            pltpu.VMEM((PLANE, 8, 128), F32),
+            pltpu.VMEM((16, 128), F32),
+            pltpu.VMEM((16, 128), F32),
+            pltpu.VMEM((16, 128), F32),
             pltpu.VMEM((PLANE, 16, 128), BF16),
             pltpu.VMEM((PLANE, 16, 128), BF16),
             pltpu.VMEM((8, 128), F32),
             pltpu.VMEM((16, 8, 128), F32),
             pltpu.VMEM((8, 128), F32),
             dma((4,)),
-            dma((4,)),
             dma((2,)),
             dma((6,)),
         ]
-        + [dma(())] * 7,
+        + [dma(())] * 6
+        + [pltpu.SemaphoreType.REGULAR],
         compiler_params=pltpu.CompilerParams(
             collective_id=0, has_side_effects=True, vmem_limit_bytes=vmem_limit
         ),
-    )(query_rows, key_rows, value_rows, grad_rows, residues.T, decay_rates.T)
-    vmem_spec = pl.BlockSpec(memory_space=pltpu.VMEM)
+    )(
+        *(
+            pltpu.with_memory_space_constraint(x, pltpu.HBM)
+            for x in (query_rows, key_rows, value_rows, grad_rows, residues.T, decay_rates.T)
+        )
+    )
     op, gq, gk, gv, gres, grate = pl.pallas_call(
         hand_over,
         out_shape=(wide, wide, wide, wide, small, small),
-        in_specs=[any_spec] * 5,
-        out_specs=[any_spec] * 4 + [vmem_spec] * 2,
-        scratch_shapes=[whole] * 4 + [pltpu.VMEM((PLANE, 8, 128), F32), dma((5,)), dma((4,))],
+        in_specs=[vmem_spec] * 5,
+        out_specs=[any_spec] * 6,
+        scratch_shapes=[pltpu.VMEM((MODES, 512), F32)] * 2 + [dma((6,))],
         compiler_params=pltpu.CompilerParams(vmem_limit_bytes=vmem_limit),
     )(*outs)
     return op, gq, gk, gv, gres.T, grate.T

time: 35 us -> 28.7 us (0.82)
  Pallas kernels: 34.2 us -> 27.9 us
    pallas_call x1, Pallas kernels: 31.4 us -> 26.9 us  [per_device(): pl.pallas_call(kernel, out_shape=(whole, whole, whole, whole, pltpu.VMEM(...]
    pallas_call x1, Pallas kernels: 2.81 us -> 1.03 us  [per_device(): pl.pallas_call(hand_over, out_shape=(wide, wide, wide, wide, small, small...]
where the time goes in v3:
time: 28.7 us; the launch traced here: 28.6 us
  Pallas kernels  27.9 us (97%)
  between operations  0.64 us (2%)
    pallas_call x1, Pallas kernels, per_device(): pl.pallas_call(kernel, out_shape=(whole, whole, whole, whole, pltpu.VMEM(...  26.9 us
    pallas_call x1, Pallas kernels, per_device(): pl.pallas_call(hand_over, out_shape=(wide, wide, wide, wide, small, small...  1.03 us

profile of v3, /device:TPU:1, one launch (start us, length us, event | category | flops | bytes accessed | tf_op | source)
XLA Modules:
  0.0 28.6 jit_solution(16892851939420376069)
XLA Ops:
  0.6 26.9 %shard_map.109 = (bf16[128,1024]{1,0:T(8,128)(2,1)S(1)}, bf16[128,1024]{1,0:T(8,128)(2,1)S(1)}, bf16[128,1024]{1,0:T(8,128)(2,1)S(1)}, bf16[128,1024]{1,0:T(8,128)(2,1)S(1)}, f32[16,8,128]{2,1,0:T(8,128)S(1)}) custom-call(bf16[128,1024]{1,0:T(8,128)(2,1)} %q_hbm.1, bf16[128,1024]{1,0:T(8,128)(2,1)} %k_hbm.1, bf16[128,1024]{1,0:T(8,128)(2,1)} %v_hbm.1, ...), custom_call_target="tpu_custom_call" | custom-call | tf_op jit(solution)/shard_map/pallas_call | solution.py:437
  27.5 1.0 %shard_map.110 = (bf16[128,1024]{1,0:T(8,128)(2,1)}, bf16[128,1024]{1,0:T(8,128)(2,1)}, bf16[128,1024]{1,0:T(8,128)(2,1)}, bf16[128,1024]{1,0:T(8,128)(2,1)}, f32[16,512]{1,0:T(8,128)}, /*index=5*/f32[16,512]{1,0:T(8,128)}) custom-call(bf16[128,1024]{1,0:T(8,128)(2,1)S(1)} %get-tuple-element.17.op_v, bf16[128,1024]{1,0:T(8,128)(2,1)S(1)} %get-tuple-element.18.gq_v, ...), custom_call_target="tpu_custom_call" | custom-call | tf_op jit(solution)/shard_map/pallas_call | solution.py:480

commit v4 on v3

v4 whole, which is shorter than its diff:
```python
import functools

import jax
import jax.numpy as jnp
from jax import lax
from jax.experimental import pallas as pl
from jax.experimental.pallas import tpu as pltpu
from jax.sharding import PartitionSpec as P

MESH = pl.DeviceIdType.MESH
F32 = jnp.float32
BF16 = jnp.bfloat16
EXACT = lax.Precision.HIGHEST

TOK = 128
CHUNKS = 8
PER = 8
GROUP = 16
MODES = 16
PLANE = 16
OWNERS = [4 * (k // 3) + k % 3 for k in range(CHUNKS)]
EARLY_FIRST = sorted(range(PLANE), key=lambda spot: spot // 4 + spot % 4)


def iota(shape, dim):
    return lax.broadcasted_iota(jnp.int32, shape, dim)


def dot(a, b, precision=None):
    return lax.dot_general(
        a, b, (((1,), (0,)), ((), ())), precision=precision, preferred_element_type=F32
    )


def dot_nt(a, b):
    return lax.dot_general(a, b, (((1,), (1,)), ((), ())), preferred_element_type=F32)


def kernel(
    q_hbm, k_hbm, v_hbm, g_hbm, res_hbm, rate_hbm,
    op_ref, gq_ref, gk_ref, gv_ref, grads_ref,
    q_v, k_v, v_v, g_v, par, wst, hrev, acoef, rhs, local, lagrev,
    send1, recv1, gsend, grecv, zsend, zrecv, wsend, wrecv, passing,
    send2, recv2, xsend, xrecv, ysend,
    in_sem, par_sem, send_sem,
    recv1_sem, recvg_sem, recvz_sem, recvw_sem, recv2_sem, recvx_sem, recvy_sem, ready_sem,
):
    ctx = lax.axis_index("ctx")
    tau = lax.axis_index("tensor")
    plane = ctx // PLANE
    me = ctx % PLANE
    z = plane * 4 + tau // 2
    core = tau % 2
    base = plane * PLANE
    first = plane == 0
    second = plane == 1
    x, y = me // 4, me % 4
    own_chunk = 3 * x + y
    owner = jnp.logical_and(jnp.logical_and(x < 3, y < 3), own_chunk < CHUNKS)
    plain = jnp.logical_not(owner)
    first_owner = jnp.logical_and(first, owner)
    second_owner = jnp.logical_and(second, owner)

    def arrived(ref, count, sem):
        pltpu.make_async_copy(ref.at[pl.ds(0, count)], ref.at[pl.ds(0, count)], sem).wait()

    def arrived_from_owners(ref, sem):
        @pl.when(owner)
        def _():
            arrived(ref, CHUNKS - 1, sem)

        @pl.when(plain)
        def _():
            arrived(ref, CHUNKS, sem)

    def send(src, dst, kind, recv_sem, device):
        pltpu.make_async_remote_copy(
            src_ref=src,
            dst_ref=dst,
            send_sem=send_sem.at[kind],
            recv_sem=recv_sem,
            device_id=device,
            device_id_type=MESH,
        ).start()

    def signal(device):
        pl.semaphore_signal(barrier, inc=1, device_id=device, device_id_type=MESH)

    barrier = pltpu.get_barrier_semaphore()

    @pl.when(owner)
    def _():
        @pl.loop(1, PLANE)
        def _(i):
            signal({"ctx": base + (me + i) % PLANE})

        @pl.loop(1, 8)
        def _(i):
            signal({"tensor": (tau + i) % 8})

    @pl.when(first_owner)
    def _():
        @pl.loop(0, 8)
        def _(i):
            signal({"ctx": PLANE + me, "tensor": (tau + i) % 8})

    lanes = pl.ds(pl.multiple_of((tau // 2) * 128, 128), 128)
    par_copies = [
        pltpu.make_async_copy(res_hbm.at[:, lanes], par.at[0], par_sem.at[0]),
        pltpu.make_async_copy(rate_hbm.at[:, lanes], par.at[1], par_sem.at[1]),
    ]
    in_copies = [
        pltpu.make_async_copy(src, dst, in_sem.at[i])
        for i, (src, dst) in enumerate(((q_hbm, q_v), (k_hbm, k_v), (g_hbm, g_v), (v_hbm, v_v)))
    ]
    for copy in par_copies + in_copies:
        copy.start()

    for copy in par_copies:
        copy.wait()

    lane16 = iota((MODES, 128), 1)
    odd = (tau % 2) == 1

    def own_half(x):
        rolled = pltpu.roll(x, 64, 1)
        first = jnp.where(odd, rolled, x)
        return jnp.where(lane16 < 64, first, jnp.where(odd, x, rolled))

    res_t = own_half(par[0])
    rate_t = own_half(par[1])

    behind = (127 - lane16).astype(F32)
    ahead = (lane16 + 1).astype(F32)

    for k in range(CHUNKS):
        for i in range(PER):
            f = k * PER + i
            decay = jnp.exp(-rate_t[:, f : f + 1] * behind)
            wst[f, 0:16, :] = decay.astype(BF16)
            wst[f, 16:32, :] = (decay * behind).astype(BF16)

    for copy in in_copies:
        copy.wait()

    turn = (iota((TOK, TOK), 0) + iota((TOK, TOK), 1) == TOK - 1).astype(BF16)
    group_of = (iota((1, 256), 1) % 128) // GROUP

    for k in range(CHUNKS):
        cols = slice(128 * k, 128 * k + 128)
        rhs[k, :, 0:128] = (q_v[:, cols].astype(F32) * k_v[:, cols].astype(F32)).astype(BF16)
        dz = (g_v[:, cols].astype(F32) * v_v[:, cols].astype(F32)).astype(BF16)
        rhs[k, :, 128:256] = dot(turn, dz).astype(BF16)

    for k in range(CHUNKS):
        weights = wst[pl.ds(k * PER, PER)].reshape(PER * 32, TOK)
        ends = dot(weights, rhs[k])
        total = jnp.zeros((32, 256), F32)
        for i in range(PER):
            total = jnp.where(group_of == i, ends[32 * i : 32 * i + 32], total)
        toward = jnp.where(first, total[:, 0:128], total[:, 128:256])
        away = jnp.where(first, total[:, 128:256], total[:, 0:128])
        send1[k] = jnp.concatenate(
            [toward[0:16], away[0:16], toward[16:32], away[16:32]], axis=0
        ).astype(BF16)

    @pl.when(plain)
    def _():
        pl.semaphore_wait(barrier, CHUNKS)

    @pl.when(first_owner)
    def _():
        pl.semaphore_wait(barrier, CHUNKS - 1 + 7)

    partner = {"ctx": (1 - plane) * PLANE + me}

    @pl.when(second_owner)
    def _():
        pl.semaphore_wait(barrier, CHUNKS - 1 + 7 + 8)

        @pl.loop(0, 8)
        def _(i):
            pl.semaphore_signal(
                ready_sem,
                inc=1,
                device_id={"ctx": me, "tensor": (tau + i) % 8},
                device_id_type=MESH,
            )

    def place(m):
        return jnp.where(first, m, PLANE - 1 - m)

    for k, peer in enumerate(OWNERS):

        @pl.when(me != peer)
        def _():
            send(send1.at[k], recv1.at[place(me)], 0, recv1_sem, {"ctx": base + peer})

        @pl.when(me == peer)
        def _():
            recv1[place(me)] = send1[k]

    row = iota((TOK, TOK), 0)
    lane = iota((TOK, TOK), 1)

    @pl.loop(0, CHUNKS, unroll=True)
    def _(k):
        u = rhs[k, :, 0:128]
        dz = rhs[k, :, 128:256]
        for i in range(PER):
            mine = jnp.where(group_of[:, 0:128] == i, dz, jnp.zeros_like(dz))
            pairs = dot_nt(mine, u)
            diag = pltpu.roll(pairs, 0, 1, stride=1, stride_axis=0)
            lagrev[k, i : i + 1, :] = jnp.sum(
                jnp.where(lane >= row, diag, 0.0), axis=0, keepdims=True
            )

    lag_all = lagrev[...].reshape(64, 128).astype(BF16)
    lag_all = jnp.concatenate([lag_all, lag_all], axis=0)
    lane_filter = iota((32, 128), 1)
    kind_filter = jnp.where(iota((32, 128), 0) < 16, lane_filter, lane_filter - 64)

    def add_filter(k, total):
        part = dot_nt(wst[pl.ds(k * PER, PER)].reshape(PER * 32, TOK), lag_all)
        for i in range(PER):
            total = jnp.where(kind_filter == k * PER + i, part[32 * i : 32 * i + 32], total)
        return total

    local_sums = lax.fori_loop(0, CHUNKS, add_filter, jnp.zeros((32, 128), F32), unroll=True)
    local_sums = local_sums[0:16] + local_sums[16:32]
    local_sums = jnp.where(lane16 < 64, local_sums, -res_t * local_sums)
    gsend[...] = local_sums
    for peer in OWNERS:

        @pl.when(me != peer)
        def _():
            send(gsend, grecv.at[me], 1, recvg_sem, {"ctx": base + peer})

    @pl.when(owner)
    def _():
        grecv[me] = gsend[...]

    for k in range(CHUNKS):
        powers = []
        for i in range(PER):
            f = k * PER + i
            rate = rate_t[:, f : f + 1]
            res = res_t[:, f : f + 1]
            decay = res * jnp.exp(-rate * behind)
            hrev[k, i : i + 1, :] = jnp.sum(decay, axis=0, keepdims=True)
            powers.append(res * jnp.exp(-rate * ahead))
        acoef[k] = jnp.concatenate(powers, axis=0).T.astype(BF16)

    @pl.loop(0, CHUNKS, unroll=True)
    def _(k):
        both = rhs[k]
        total = jnp.zeros((TOK, 256), F32)
        for i in range(PER):
            taps = pltpu.roll(
                jnp.broadcast_to(hrev[k, i : i + 1, :], (TOK, TOK)), 1, 1, stride=1, stride_axis=0
            )
            taps = jnp.where(lane <= row, taps, 0.0).astype(BF16)
            total = jnp.where(group_of == i, dot(taps, both), total)
        local[k] = total

    @pl.when(owner)
    def _():
        spread = (iota((128, 128), 0) == PER * own_chunk + iota((128, 128), 1) // GROUP).astype(F32)
        rate_spread = dot(rate_t, spread, EXACT)
        res_spread = dot(res_t, spread, EXACT)
        step = jnp.exp(-rate_spread * float(TOK))
        single = jnp.exp(-rate_spread)
        collect = (iota((128, 128), 1) % 64 == 8 * tau + iota((128, 128), 0) // GROUP).astype(BF16)
        zero = jnp.zeros((MODES, 128), F32)

        arrived(recv1, PLANE - 1, recv1_sem)

        away_ends, states = [], []
        one, two, sum_one, sum_two = zero, zero, zero, zero
        lag = float(TOK) * step
        for i in range(PLANE):
            block = recv1[i].astype(F32)
            toward_one, away_one, toward_two, away_two = (
                block[16 * part : 16 * part + 16] for part in range(4)
            )
            away_ends.append(away_one)
            states.append(one)
            sum_one = sum_one + one * away_one
            sum_two = sum_two + (two * away_one + one * (away_two + away_one))
            two = step * two + (lag * one + toward_two)
            one = step * one + toward_one

        def collected(one_sum, two_sum):
            one_sum, two_sum = single * one_sum, -res_spread * single * two_sum
            one_high, two_high = one_sum.astype(BF16), two_sum.astype(BF16)
            parts = jnp.concatenate(
                [
                    one_high.astype(F32),
                    one_sum - one_high.astype(F32),
                    two_high.astype(F32),
                    two_sum - two_high.astype(F32),
                ],
                axis=0,
            ).astype(BF16)
            parts = dot(parts, collect)
            return jnp.where(lane16 < 64, parts[0:16] + parts[16:32], parts[32:48] + parts[48:64])

        def within_plane():
            arrived(grecv, PLANE - 1, recvg_sem)
            inside = jnp.where((lane16 % 64) // PER == own_chunk, jnp.sum(grecv[...], axis=0), 0.0)
            inside = pltpu.roll(inside, (128 + PER * (tau - own_chunk)) % 128, 1)
            return inside + collected(sum_one, sum_two)

        def send_along_z(grads):
            xsend[...] = grads.astype(BF16)
            for there in range(8):
                for other in (1, 0):
                    device = {"ctx": (there // 4) * PLANE + me, "tensor": (there % 4) * 2 + other}

                    @pl.when(jnp.logical_or(z != there, core != other))
                    def _():
                        send(xsend, xrecv.at[plane * 8 + tau], 4, recvx_sem, device)

            xrecv[plane * 8 + tau] = grads.astype(BF16)

        @pl.when(first)
        def _():
            zsend[0:16] = one
            zsend[16:32] = two
            pl.semaphore_wait(ready_sem, 8)
            send(zsend, zrecv, 3, recvz_sem, partner)
            send_along_z(within_plane())

        @pl.when(second)
        def _():
            wsend[...] = one
            send(wsend, wrecv, 3, recvw_sem, partner)
            grads = within_plane()
            pltpu.make_async_copy(zrecv, zrecv, recvz_sem).wait()
            other_one, other_two = zrecv[0:16], zrecv[16:32]
            passing[...] = other_one
            send_along_z(
                grads
                + collected(one * other_one, two * other_one + one * (other_two + other_one))
            )

        @pl.when(first)
        def _():
            pltpu.make_async_copy(wrecv, wrecv, recvw_sem).wait()
            passing[...] = wrecv[...]

        passed = passing[...]
        away = zero
        for i in reversed(range(PLANE)):
            toward, beside = states[i], away + passed
            send2[i] = jnp.concatenate(
                [jnp.where(first, toward, beside), jnp.where(first, beside, toward)], axis=0
            ).astype(BF16)
            away = step * away + away_ends[i]
            passed = step * passed
        for peer in EARLY_FIRST:

            @pl.when(me != peer)
            def _():
                send(send2.at[place(peer)], recv2.at[own_chunk], 2, recv2_sem, {"ctx": base + peer})

        recv2[own_chunk] = send2[place(me)]

        arrived(xrecv, 15, recvx_sem)
        total = jnp.sum(xrecv[...].astype(F32), axis=0).astype(BF16)
        ysend[...] = total
        for peer in EARLY_FIRST:

            @pl.when(me != peer)
            def _():
                send(ysend, grads_ref.at[own_chunk], 5, recvy_sem, {"ctx": base + peer})

        grads_ref[own_chunk] = total

    arrived_from_owners(recv2, recv2_sem)

    block_diagonal = (iota((PER, MODES, 256), 2) % 128) // GROUP == iota((PER, MODES, 256), 0)

    @pl.loop(0, CHUNKS, unroll=True)
    def _(k):
        cols = pl.ds(pl.multiple_of(k * 128, 128), 128)
        block = recv2[k]
        states = jnp.concatenate([block[0:16], block[16:32]], axis=1).astype(F32)
        states = jnp.where(block_diagonal, states[None], 0.0).reshape(PER * MODES, 256)
        total = local[k] + dot(acoef[k], states.astype(BF16))
        conv = total[:, 0:128].astype(BF16).astype(F32)
        back = dot(turn, total[:, 128:256].astype(BF16))
        op_ref[:, cols] = (v_v[:, cols].astype(F32) * conv).astype(BF16)
        gv_ref[:, cols] = (g_v[:, cols].astype(F32) * conv).astype(BF16)
        gq_ref[:, cols] = (k_v[:, cols].astype(F32) * back).astype(BF16)
        gk_ref[:, cols] = (q_v[:, cols].astype(F32) * back).astype(BF16)

    arrived_from_owners(send1, send_sem.at[0])
    arrived_from_owners(grecv, send_sem.at[1])

    @pl.when(first_owner)
    def _():
        pltpu.make_async_copy(zsend, zsend, send_sem.at[3]).wait()

    @pl.when(second_owner)
    def _():
        pltpu.make_async_copy(wsend, wsend, send_sem.at[3]).wait()

    @pl.when(owner)
    def _():
        arrived(send2, PLANE - 1, send_sem.at[2])
        arrived(xrecv, 15, send_sem.at[4])
        arrived(xrecv, PLANE - 1, send_sem.at[5])

    arrived_from_owners(grads_ref, recvy_sem)


def hand_over(
    op_v, gq_v, gk_v, gv_v, grads_v,
    op_out, gq_out, gk_out, gv_out, gres_out, grate_out,
    gres_v, grate_v, out_sem,
):
    held = (op_v, gq_v, gk_v, gv_v, gres_v, grate_v)
    results = (op_out, gq_out, gk_out, gv_out, gres_out, grate_out)
    out = [pltpu.make_async_copy(held[i], results[i], out_sem.at[i]) for i in range(6)]
    for copy in out[:4]:
        copy.start()

    lane = iota((MODES, 128), 1)
    rows = [
        grads_v[k].astype(F32) for k in range(CHUNKS)
    ]
    for bit in (4, 2, 1):
        clear = (lane // PER) % (2 * bit) < bit
        turned = list(rows)
        for k in range(CHUNKS):
            if k & bit:
                continue
            near, far = rows[k], rows[k + bit]
            turned[k] = jnp.where(clear, near, pltpu.roll(far, PER * bit, 1))
            turned[k + bit] = jnp.where(clear, pltpu.roll(near, 128 - PER * bit, 1), far)
        rows = turned
    for j in range(4):
        even, uneven = rows[2 * j], rows[2 * j + 1]
        gres_v[:, 128 * j : 128 * j + 128] = jnp.where(
            lane < 64, even, pltpu.roll(uneven, 64, 1)
        )
        grate_v[:, 128 * j : 128 * j + 128] = jnp.where(
            lane < 64, pltpu.roll(even, 64, 1), uneven
        )
    out[4].start()
    out[5].start()

    for copy in out:
        copy.wait()


def per_device(query_rows, key_rows, value_rows, grad_rows, residues, decay_rates):
    rows, width = query_rows.shape
    any_spec = pl.BlockSpec(memory_space=pl.ANY)
    vmem_spec = pl.BlockSpec(memory_space=pltpu.VMEM)
    vmem_limit = 16 * 1024 * 1024
    wide = jax.ShapeDtypeStruct((rows, width), BF16)
    small = jax.ShapeDtypeStruct((MODES, 512), F32)
    dma = pltpu.SemaphoreType.DMA
    whole = pltpu.VMEM((rows, width), BF16)
    outs = pl.pallas_call(
        kernel,
        out_shape=(whole, whole, whole, whole, pltpu.VMEM((CHUNKS, MODES, 128), BF16)),
        in_specs=[any_spec] * 6,
        out_specs=[vmem_spec] * 5,
        scratch_shapes=[whole] * 4
        + [
            pltpu.VMEM((2, MODES, 128), F32),
            pltpu.VMEM((64, 32, 128), BF16),
            pltpu.VMEM((CHUNKS, PER, 128), F32),
            pltpu.VMEM((CHUNKS, TOK, 128), BF16),
            pltpu.VMEM((CHUNKS, TOK, 256), BF16),
            pltpu.VMEM((CHUNKS, TOK, 256), F32),
            pltpu.VMEM((CHUNKS, PER, 128), F32),
            pltpu.VMEM((CHUNKS, 64, 128), BF16),
            pltpu.VMEM((PLANE, 64, 128), BF16),
            pltpu.VMEM((MODES, 128), F32),
            pltpu.VMEM((PLANE, MODES, 128), F32),
            pltpu.VMEM((32, 128), F32),
            pltpu.VMEM((32, 128), F32),
            pltpu.VMEM((MODES, 128), F32),
            pltpu.VMEM((MODES, 128), F32),
            pltpu.VMEM((MODES, 128), F32),
            pltpu.VMEM((PLANE, 32, 128), BF16),
            pltpu.VMEM((CHUNKS, 32, 128), BF16),
            pltpu.VMEM((MODES, 128), BF16),
            pltpu.VMEM((16, MODES, 128), BF16),
            pltpu.VMEM((MODES, 128), BF16),
            dma((4,)),
            dma((2,)),
            dma((6,)),
        ]
        + [dma(())] * 7
        + [pltpu.SemaphoreType.REGULAR],
        compiler_params=pltpu.CompilerParams(
            collective_id=0, has_side_effects=True, vmem_limit_bytes=vmem_limit
        ),
    )(
        *(
            pltpu.with_memory_space_constraint(x, pltpu.HBM)
            for x in (query_rows, key_rows, value_rows, grad_rows, residues.T, decay_rates.T)
        )
    )
    op, gq, gk, gv, gres, grate = pl.pallas_call(
        hand_over,
        out_shape=(wide, wide, wide, wide, small, small),
        in_specs=[vmem_spec] * 5,
        out_specs=[any_spec] * 6,
        scratch_shapes=[pltpu.VMEM((MODES, 512), F32)] * 2 + [dma((6,))],
        compiler_params=pltpu.CompilerParams(vmem_limit_bytes=vmem_limit),
    )(*outs)
    return op, gq, gk, gv, gres.T, grate.T


def solution(mesh):
    wide = P("ctx", "tensor")
    return jax.shard_map(
        per_device,
        mesh=mesh,
        in_specs=(wide, wide, wide, wide, P(), P()),
        out_specs=(wide, wide, wide, wide, P(), P()),
        check_vma=False,
    )
```

time: 28.7 us -> 27.9 us (0.972)
  Pallas kernels: 27.9 us -> 27 us
    pallas_call x1, Pallas kernels: 26.9 us -> 25.9 us  [per_device(): pl.pallas_call(kernel, out_shape=(whole, whole, whole, whole, pltpu.VMEM(...]
where the time goes in v4:
time: 27.9 us; the launch traced here: 27.6 us
  Pallas kernels  27 us (97%)
  between operations  0.64 us (2%)
    pallas_call x1, Pallas kernels, per_device(): pl.pallas_call(kernel, out_shape=(whole, whole, whole, whole, pltpu.VMEM(...  25.9 us
    pallas_call x1, Pallas kernels, per_device(): pl.pallas_call(hand_over, out_shape=(wide, wide, wide, wide, small, small...  1.03 us

profile of v4, /device:TPU:1, one launch (start us, length us, event | category | flops | bytes accessed | tf_op | source)
XLA Modules:
  0.0 27.6 jit_solution(9866410250296570377)
XLA Ops:
  0.6 25.9 %shard_map.109 = (bf16[128,1024]{1,0:T(8,128)(2,1)S(1)}, bf16[128,1024]{1,0:T(8,128)(2,1)S(1)}, bf16[128,1024]{1,0:T(8,128)(2,1)S(1)}, bf16[128,1024]{1,0:T(8,128)(2,1)S(1)}, bf16[8,16,128]{2,1,0:T(8,128)(2,1)S(1)}) custom-call(bf16[128,1024]{1,0:T(8,128)(2,1)} %q_hbm.1, bf16[128,1024]{1,0:T(8,128)(2,1)} %k_hbm.1, bf16[128,1024]{1,0:T(8,128)(2,1)} %v_hbm.1, ...), custom_call_target="tpu_custom_call" | custom-call | tf_op jit(solution)/shard_map/pallas_call | solution.py:467
  26.6 1.0 %shard_map.110 = (bf16[128,1024]{1,0:T(8,128)(2,1)}, bf16[128,1024]{1,0:T(8,128)(2,1)}, bf16[128,1024]{1,0:T(8,128)(2,1)}, bf16[128,1024]{1,0:T(8,128)(2,1)}, f32[16,512]{1,0:T(8,128)}, /*index=5*/f32[16,512]{1,0:T(8,128)}) custom-call(bf16[128,1024]{1,0:T(8,128)(2,1)S(1)} %get-tuple-element.17.op_v, bf16[128,1024]{1,0:T(8,128)(2,1)S(1)} %get-tuple-element.18.gq_v, ...), custom_call_target="tpu_custom_call" | custom-call | tf_op jit(solution)/shard_map/pallas_call | solution.py:510

commit v5 on v4

--- a/solution.py
+++ b/solution.py
@@ -18,7 +18,7 @@
 GROUP = 16
 MODES = 16
 PLANE = 16
-OWNERS = [4 * (k // 3) + k % 3 for k in range(CHUNKS)]
+OWNERS = [4 * (k // 2) + k % 2 for k in range(CHUNKS)]
 EARLY_FIRST = sorted(range(PLANE), key=lambda spot: spot // 4 + spot % 4)
 
 
@@ -55,8 +55,8 @@
     first = plane == 0
     second = plane == 1
     x, y = me // 4, me % 4
-    own_chunk = 3 * x + y
-    owner = jnp.logical_and(jnp.logical_and(x < 3, y < 3), own_chunk < CHUNKS)
+    own_chunk = 2 * x + y
+    owner = y < 2
     plain = jnp.logical_not(owner)
     first_owner = jnp.logical_and(first, owner)
     second_owner = jnp.logical_and(second, owner)
@@ -152,17 +152,32 @@
         dz = (g_v[:, cols].astype(F32) * v_v[:, cols].astype(F32)).astype(BF16)
         rhs[k, :, 128:256] = dot(turn, dz).astype(BF16)
 
-    for k in range(CHUNKS):
-        weights = wst[pl.ds(k * PER, PER)].reshape(PER * 32, TOK)
-        ends = dot(weights, rhs[k])
-        total = jnp.zeros((32, 256), F32)
-        for i in range(PER):
-            total = jnp.where(group_of == i, ends[32 * i : 32 * i + 32], total)
-        toward = jnp.where(first, total[:, 0:128], total[:, 128:256])
-        away = jnp.where(first, total[:, 128:256], total[:, 0:128])
-        send1[k] = jnp.concatenate(
-            [toward[0:16], away[0:16], toward[16:32], away[16:32]], axis=0
-        ).astype(BF16)
+    def end_states(chunks):
+        for k in chunks:
+            weights = wst[pl.ds(k * PER, PER)].reshape(PER * 32, TOK)
+            ends = dot(weights, rhs[k])
+            total = jnp.zeros((32, 256), F32)
+            for i in range(PER):
+                total = jnp.where(group_of == i, ends[32 * i : 32 * i + 32], total)
+            toward = jnp.where(first, total[:, 0:128], total[:, 128:256])
+            away = jnp.where(first, total[:, 128:256], total[:, 0:128])
+            send1[k] = jnp.concatenate(
+                [toward[0:16], away[0:16], toward[16:32], away[16:32]], axis=0
+            ).astype(BF16)
+
+    def send_ends(chunks):
+        for k in chunks:
+            peer = OWNERS[k]
+
+            @pl.when(me != peer)
+            def _():
+                send(send1.at[k], recv1.at[place(me)], 0, recv1_sem, {"ctx": base + peer})
+
+            @pl.when(me == peer)
+            def _():
+                recv1[place(me)] = send1[k]
+
+    end_states(range(0, 4))
 
     @pl.when(plain)
     def _():
@@ -190,15 +205,9 @@
     def place(m):
         return jnp.where(first, m, PLANE - 1 - m)
 
-    for k, peer in enumerate(OWNERS):
-
-        @pl.when(me != peer)
-        def _():
-            send(send1.at[k], recv1.at[place(me)], 0, recv1_sem, {"ctx": base + peer})
-
-        @pl.when(me == peer)
-        def _():
-            recv1[place(me)] = send1[k]
+    send_ends(range(0, 4))
+    end_states(range(4, 8))
+    send_ends(range(4, 8))
 
     row = iota((TOK, TOK), 0)
     lane = iota((TOK, TOK), 1)
@@ -229,7 +238,7 @@
     local_sums = lax.fori_loop(0, CHUNKS, add_filter, jnp.zeros((32, 128), F32), unroll=True)
     local_sums = local_sums[0:16] + local_sums[16:32]
     local_sums = jnp.where(lane16 < 64, local_sums, -res_t * local_sums)
-    gsend[...] = local_sums
+    gsend[...] = local_sums.astype(BF16)
     for peer in OWNERS:
 
         @pl.when(me != peer)
@@ -275,20 +284,30 @@
 
         arrived(recv1, PLANE - 1, recv1_sem)
 
-        away_ends, states = [], []
-        one, two, sum_one, sum_two = zero, zero, zero, zero
+        states, one, two = [], zero, zero
         lag = float(TOK) * step
         for i in range(PLANE):
-            block = recv1[i].astype(F32)
-            toward_one, away_one, toward_two, away_two = (
-                block[16 * part : 16 * part + 16] for part in range(4)
-            )
-            away_ends.append(away_one)
-            states.append(one)
-            sum_one = sum_one + one * away_one
-            sum_two = sum_two + (two * away_one + one * (away_two + away_one))
-            two = step * two + (lag * one + toward_two)
-            one = step * one + toward_one
+            states.append((one, two))
+            two = step * two + (lag * one + recv1[i, 32:48, :].astype(F32))
+            one = step * one + recv1[i, 0:16, :].astype(F32)
+
+        @pl.when(first)
+        def _():
+            zsend[0:16] = one
+            zsend[16:32] = two
+            pl.semaphore_wait(ready_sem, 8)
+            send(zsend, zrecv, 3, recvz_sem, partner)
+
+        @pl.when(second)
+        def _():
+            wsend[...] = one
+            send(wsend, wrecv, 3, recvw_sem, partner)
+
+        sum_one, sum_two = zero, zero
+        for i in range(PLANE):
+            away_one, away_two = recv1[i, 16:32, :].astype(F32), recv1[i, 48:64, :].astype(F32)
+            sum_one = sum_one + states[i][0] * away_one
+            sum_two = sum_two + (states[i][1] * away_one + states[i][0] * (away_two + away_one))
 
         def collected(one_sum, two_sum):
             one_sum, two_sum = single * one_sum, -res_spread * single * two_sum
@@ -307,7 +326,7 @@
 
         def within_plane():
             arrived(grecv, PLANE - 1, recvg_sem)
-            inside = jnp.where((lane16 % 64) // PER == own_chunk, jnp.sum(grecv[...], axis=0), 0.0)
+            inside = jnp.where((lane16 % 64) // PER == own_chunk, jnp.sum(grecv[...].astype(F32), axis=0), 0.0)
             inside = pltpu.roll(inside, (128 + PER * (tau - own_chunk)) % 128, 1)
             return inside + collected(sum_one, sum_two)
 
@@ -325,16 +344,10 @@
 
         @pl.when(first)
         def _():
-            zsend[0:16] = one
-            zsend[16:32] = two
-            pl.semaphore_wait(ready_sem, 8)
-            send(zsend, zrecv, 3, recvz_sem, partner)
             send_along_z(within_plane())
 
         @pl.when(second)
         def _():
-            wsend[...] = one
-            send(wsend, wrecv, 3, recvw_sem, partner)
             grads = within_plane()
             pltpu.make_async_copy(zrecv, zrecv, recvz_sem).wait()
             other_one, other_two = zrecv[0:16], zrecv[16:32]
@@ -352,11 +365,11 @@
         passed = passing[...]
         away = zero
         for i in reversed(range(PLANE)):
-            toward, beside = states[i], away + passed
+            toward, beside = states[i][0], away + passed
             send2[i] = jnp.concatenate(
                 [jnp.where(first, toward, beside), jnp.where(first, beside, toward)], axis=0
             ).astype(BF16)
-            away = step * away + away_ends[i]
+            away = step * away + recv1[i, 16:32, :].astype(F32)
             passed = step * passed
         for peer in EARLY_FIRST:
 
@@ -480,8 +493,8 @@
             pltpu.VMEM((CHUNKS, PER, 128), F32),
             pltpu.VMEM((CHUNKS, 64, 128), BF16),
             pltpu.VMEM((PLANE, 64, 128), BF16),
-            pltpu.VMEM((MODES, 128), F32),
-            pltpu.VMEM((PLANE, MODES, 128), F32),
+            pltpu.VMEM((MODES, 128), BF16),
+            pltpu.VMEM((PLANE, MODES, 128), BF16),
             pltpu.VMEM((32, 128), F32),
             pltpu.VMEM((32, 128), F32),
             pltpu.VMEM((MODES, 128), F32),

time: 27.9 us -> 27.3 us (0.978)
  Pallas kernels: 27 us -> 26.6 us
    pallas_call x1, Pallas kernels: 25.9 us -> 25.6 us  [per_device(): pl.pallas_call(kernel, out_shape=(whole, whole, whole, whole, pltpu.VMEM(...]
where the time goes in v5:
time: 27.3 us; the launch traced here: 27.2 us
  Pallas kernels  26.6 us (97%)
  between operations  0.64 us (2%)
    pallas_call x1, Pallas kernels, per_device(): pl.pallas_call(kernel, out_shape=(whole, whole, whole, whole, pltpu.VMEM(...  25.6 us
    pallas_call x1, Pallas kernels, per_device(): pl.pallas_call(hand_over, out_shape=(wide, wide, wide, wide, small, small...  1.03 us

profile of v5, /device:TPU:1, one launch (start us, length us, event | category | flops | bytes accessed | tf_op | source)
XLA Modules:
  0.0 27.2 jit_solution(9967209020480958037)
XLA Ops:
  0.6 25.6 %shard_map.109 = (bf16[128,1024]{1,0:T(8,128)(2,1)S(1)}, bf16[128,1024]{1,0:T(8,128)(2,1)S(1)}, bf16[128,1024]{1,0:T(8,128)(2,1)S(1)}, bf16[128,1024]{1,0:T(8,128)(2,1)S(1)}, bf16[8,16,128]{2,1,0:T(8,128)(2,1)S(1)}) custom-call(bf16[128,1024]{1,0:T(8,128)(2,1)} %q_hbm.1, bf16[128,1024]{1,0:T(8,128)(2,1)} %k_hbm.1, bf16[128,1024]{1,0:T(8,128)(2,1)} %v_hbm.1, ...), custom_call_target="tpu_custom_call" | custom-call | tf_op jit(solution)/shard_map/pallas_call | solution.py:480
  26.2 1.0 %shard_map.110 = (bf16[128,1024]{1,0:T(8,128)(2,1)}, bf16[128,1024]{1,0:T(8,128)(2,1)}, bf16[128,1024]{1,0:T(8,128)(2,1)}, bf16[128,1024]{1,0:T(8,128)(2,1)}, f32[16,512]{1,0:T(8,128)}, /*index=5*/f32[16,512]{1,0:T(8,128)}) custom-call(bf16[128,1024]{1,0:T(8,128)(2,1)S(1)} %get-tuple-element.17.op_v, bf16[128,1024]{1,0:T(8,128)(2,1)S(1)} %get-tuple-element.18.gq_v, ...), custom_call_target="tpu_custom_call" | custom-call | tf_op jit(solution)/shard_map/pallas_call | solution.py:523

commit v6 on v5

--- a/solution.py
+++ b/solution.py
@@ -293,8 +293,8 @@
 
         @pl.when(first)
         def _():
-            zsend[0:16] = one
-            zsend[16:32] = two
+            zsend[0:16] = one.astype(BF16)
+            zsend[16:32] = two.astype(BF16)
             pl.semaphore_wait(ready_sem, 8)
             send(zsend, zrecv, 3, recvz_sem, partner)
 
@@ -311,18 +311,8 @@
 
         def collected(one_sum, two_sum):
             one_sum, two_sum = single * one_sum, -res_spread * single * two_sum
-            one_high, two_high = one_sum.astype(BF16), two_sum.astype(BF16)
-            parts = jnp.concatenate(
-                [
-                    one_high.astype(F32),
-                    one_sum - one_high.astype(F32),
-                    two_high.astype(F32),
-                    two_sum - two_high.astype(F32),
-                ],
-                axis=0,
-            ).astype(BF16)
-            parts = dot(parts, collect)
-            return jnp.where(lane16 < 64, parts[0:16] + parts[16:32], parts[32:48] + parts[48:64])
+            parts = dot(jnp.concatenate([one_sum, two_sum], axis=0).astype(BF16), collect)
+            return jnp.where(lane16 < 64, parts[0:16], parts[16:32])
 
         def within_plane():
             arrived(grecv, PLANE - 1, recvg_sem)
@@ -350,7 +340,7 @@
         def _():
             grads = within_plane()
             pltpu.make_async_copy(zrecv, zrecv, recvz_sem).wait()
-            other_one, other_two = zrecv[0:16], zrecv[16:32]
+            other_one, other_two = zrecv[0:16].astype(F32), zrecv[16:32].astype(F32)
             passing[...] = other_one
             send_along_z(
                 grads
@@ -495,8 +485,8 @@
             pltpu.VMEM((PLANE, 64, 128), BF16),
             pltpu.VMEM((MODES, 128), BF16),
             pltpu.VMEM((PLANE, MODES, 128), BF16),
-            pltpu.VMEM((32, 128), F32),
-            pltpu.VMEM((32, 128), F32),
+            pltpu.VMEM((32, 128), BF16),
+            pltpu.VMEM((32, 128), BF16),
             pltpu.VMEM((MODES, 128), F32),
             pltpu.VMEM((MODES, 128), F32),
             pltpu.VMEM((MODES, 128), F32),

time: 27.3 us -> 27.2 us (level)
  no operation moved by 1% of the time
where the time goes in v6:
time: 27.2 us; the launch traced here: 27.1 us
  Pallas kernels  26.5 us (97%)
  between operations  0.64 us (2%)
    pallas_call x1, Pallas kernels, per_device(): pl.pallas_call(kernel, out_shape=(whole, whole, whole, whole, pltpu.VMEM(...  25.4 us
    pallas_call x1, Pallas kernels, per_device(): pl.pallas_call(hand_over, out_shape=(wide, wide, wide, wide, small, small...  1.03 us

profile of v6, /device:TPU:1, one launch (start us, length us, event | category | flops | bytes accessed | tf_op | source)
XLA Modules:
  0.0 27.1 jit_solution(582173384088406928)
XLA Ops:
  0.6 25.4 %shard_map.109 = (bf16[128,1024]{1,0:T(8,128)(2,1)S(1)}, bf16[128,1024]{1,0:T(8,128)(2,1)S(1)}, bf16[128,1024]{1,0:T(8,128)(2,1)S(1)}, bf16[128,1024]{1,0:T(8,128)(2,1)S(1)}, bf16[8,16,128]{2,1,0:T(8,128)(2,1)S(1)}) custom-call(bf16[128,1024]{1,0:T(8,128)(2,1)} %q_hbm.1, bf16[128,1024]{1,0:T(8,128)(2,1)} %k_hbm.1, bf16[128,1024]{1,0:T(8,128)(2,1)} %v_hbm.1, ...), custom_call_target="tpu_custom_call" | custom-call | tf_op jit(solution)/shard_map/pallas_call | solution.py:470
  26.1 1.0 %shard_map.110 = (bf16[128,1024]{1,0:T(8,128)(2,1)}, bf16[128,1024]{1,0:T(8,128)(2,1)}, bf16[128,1024]{1,0:T(8,128)(2,1)}, bf16[128,1024]{1,0:T(8,128)(2,1)}, f32[16,512]{1,0:T(8,128)}, /*index=5*/f32[16,512]{1,0:T(8,128)}) custom-call(bf16[128,1024]{1,0:T(8,128)(2,1)S(1)} %get-tuple-element.17.op_v, bf16[128,1024]{1,0:T(8,128)(2,1)S(1)} %get-tuple-element.18.gq_v, ...), custom_call_target="tpu_custom_call" | custom-call | tf_op jit(solution)/shard_map/pallas_call | solution.py:513

commit v7 on v6

--- a/solution.py
+++ b/solution.py
@@ -293,8 +293,8 @@
 
         @pl.when(first)
         def _():
-            zsend[0:16] = one.astype(BF16)
-            zsend[16:32] = two.astype(BF16)
+            zsend[0:16] = one
+            zsend[16:32] = two
             pl.semaphore_wait(ready_sem, 8)
             send(zsend, zrecv, 3, recvz_sem, partner)
 
@@ -340,7 +340,7 @@
         def _():
             grads = within_plane()
             pltpu.make_async_copy(zrecv, zrecv, recvz_sem).wait()
-            other_one, other_two = zrecv[0:16].astype(F32), zrecv[16:32].astype(F32)
+            other_one, other_two = zrecv[0:16], zrecv[16:32]
             passing[...] = other_one
             send_along_z(
                 grads
@@ -485,8 +485,8 @@
             pltpu.VMEM((PLANE, 64, 128), BF16),
             pltpu.VMEM((MODES, 128), BF16),
             pltpu.VMEM((PLANE, MODES, 128), BF16),
-            pltpu.VMEM((32, 128), BF16),
-            pltpu.VMEM((32, 128), BF16),
+            pltpu.VMEM((32, 128), F32),
+            pltpu.VMEM((32, 128), F32),
             pltpu.VMEM((MODES, 128), F32),
             pltpu.VMEM((MODES, 128), F32),
             pltpu.VMEM((MODES, 128), F32),

time: 27.2 us -> 27.3 us (level)
  no operation moved by 1% of the time
where the time goes in v7:
time: 27.3 us; the launch traced here: 27.2 us
  Pallas kernels  26.6 us (97%)
  between operations  0.64 us (2%)
    pallas_call x1, Pallas kernels, per_device(): pl.pallas_call(kernel, out_shape=(whole, whole, whole, whole, pltpu.VMEM(...  25.6 us
    pallas_call x1, Pallas kernels, per_device(): pl.pallas_call(hand_over, out_shape=(wide, wide, wide, wide, small, small...  1.03 us

profile of v7, /device:TPU:1, one launch (start us, length us, event | category | flops | bytes accessed | tf_op | source)
XLA Modules:
  0.0 27.2 jit_solution(11017617703933385774)
XLA Ops:
  0.6 25.6 %shard_map.109 = (bf16[128,1024]{1,0:T(8,128)(2,1)S(1)}, bf16[128,1024]{1,0:T(8,128)(2,1)S(1)}, bf16[128,1024]{1,0:T(8,128)(2,1)S(1)}, bf16[128,1024]{1,0:T(8,128)(2,1)S(1)}, bf16[8,16,128]{2,1,0:T(8,128)(2,1)S(1)}) custom-call(bf16[128,1024]{1,0:T(8,128)(2,1)} %q_hbm.1, bf16[128,1024]{1,0:T(8,128)(2,1)} %k_hbm.1, bf16[128,1024]{1,0:T(8,128)(2,1)} %v_hbm.1, ...), custom_call_target="tpu_custom_call" | custom-call | tf_op jit(solution)/shard_map/pallas_call | solution.py:470
  26.2 1.0 %shard_map.110 = (bf16[128,1024]{1,0:T(8,128)(2,1)}, bf16[128,1024]{1,0:T(8,128)(2,1)}, bf16[128,1024]{1,0:T(8,128)(2,1)}, bf16[128,1024]{1,0:T(8,128)(2,1)}, f32[16,512]{1,0:T(8,128)}, /*index=5*/f32[16,512]{1,0:T(8,128)}) custom-call(bf16[128,1024]{1,0:T(8,128)(2,1)S(1)} %get-tuple-element.17.op_v, bf16[128,1024]{1,0:T(8,128)(2,1)S(1)} %get-tuple-element.18.gq_v, ...), custom_call_target="tpu_custom_call" | custom-call | tf_op jit(solution)/shard_map/pallas_call | solution.py:513
